TPU v7x, 256 devices: a whole 4x4x8 slice. The times are simulated.
256 devices in a mesh: slab: 16 (over y, x), expert: 16 (over z, core).
Axes of the slice: x: 4, y: 4, z: 8, core: 2. Of those that a mesh axis runs over, the one named last changes fastest.
Arguments:
- features: bfloat16 [32, 32, 128, 128], P(None, 'slab', 'expert'), may hold values from -6 to 6
- kernel: bfloat16 [27, 32, 32], replicated, may hold values from -0.21875 to 0.21875
- labels: int32 [32, 128, 128], P('slab', 'expert'), may hold values from 0 to 116
- region_ids: int32 [16, 16, 16, 1], P('slab', 'expert'), may hold values from 0 to 15; in each aligned block of 16 rows (0 to 15, 16 to 31, ..., all dimensions but the last counted through in order) at most 2 rows name the same one
- first_weight: bfloat16 [16, 256, 32], P('expert'), may hold values from -1 to 1
- first_bias: bfloat16 [16, 256], P('expert'), may hold values from -3 to 3
- second_weight: bfloat16 [16, 117, 256], P('expert'), may hold values from -0.375 to 0.375
- second_bias: bfloat16 [16, 117], P('expert'), may hold values from -3 to 3
Outputs:
- loss: float32 [], replicated
- grad_kernel: float32 [27, 32, 32], replicated
- grad_first_weight: float32 [16, 256, 32], P('expert')
- grad_first_bias: float32 [16, 256], P('expert')
- grad_second_weight: float32 [16, 117, 256], P('expert')
- grad_second_bias: float32 [16, 117], P('expert')
Inputs may be any that keep to these rules, and one draw needn't show every extreme that they name: `region_ids`: within the rows of one device no expert is named by more than 2 rows, and in some device one expert is named by exactly 2 rows.
All inputs are finite; a program needn't handle non-finite values.
Results may differ from a plain program's by a relative error of at most 0.013.
Values may be sent and summed in bfloat16 or wider, within the bound.
A program may use at most 64 MiB of HBM per device.

v0:
```python
import math

import jax
import jax.numpy as jnp
from jax import lax
from jax.sharding import PartitionSpec as P


def with_halo(x, sides, width):
    for axis, dim in sides:
        peers, length = (lax.axis_size(axis), x.shape[dim])
        up = [(i, (i + 1) % peers) for i in range(peers - 1)]
        down = [(j, i) for i, j in up]
        last = lax.slice_in_dim(x, length - width, length, axis=dim)
        initial = lax.slice_in_dim(x, 0, width, axis=dim)
        before = lax.ppermute(last, axis, up)
        after = lax.ppermute(initial, axis, down)
        x = jnp.concatenate([before, x, after], axis=dim)
    return x


def silu_grad(pre_value):
    sigmoid_value = jax.nn.sigmoid(pre_value)
    return sigmoid_value * (1.0 + pre_value * (1.0 - sigmoid_value))


def shifted(padded, tap_index, depth_cells, height_cells, width_cells):
    offset_z = tap_index // 9
    offset_h = tap_index % 9 // 3
    offset_w = tap_index % 3
    return padded[
        :,
        offset_z : offset_z + depth_cells,
        offset_h : offset_h + height_cells,
        offset_w : offset_w + width_cells,
    ]


def expert_forward(inputs, weight_one, bias_one, weight_two, bias_two):
    hidden_pre = (
        jnp.einsum("bhc,bcn->bhn", weight_one, inputs, preferred_element_type=jnp.float32)
        + bias_one.astype(jnp.float32)[:, :, None]
    )
    hidden_act = jax.nn.silu(hidden_pre).astype(jnp.bfloat16)
    logits = (
        jnp.einsum("bkh,bhn->bkn", weight_two, hidden_act, preferred_element_type=jnp.float32)
        + bias_two.astype(jnp.float32)[:, :, None]
    )
    return (hidden_pre, hidden_act, logits.astype(jnp.bfloat16))


def class_sums(logits, labels_block):
    probs = jax.nn.sigmoid(logits.astype(jnp.float32))
    classes = lax.broadcasted_iota(jnp.int32, (1, logits.shape[1], 1), 1)
    onehot = (labels_block[:, None, :] == classes).astype(jnp.float32)
    live = (labels_block >= 0).astype(jnp.float32)[:, None, :]
    return jnp.stack(
        [
            jnp.sum(probs * onehot, axis=(0, 2)),
            jnp.sum(probs * live, axis=(0, 2)),
            jnp.sum(onehot, axis=(0, 2)),
        ]
    )


def expert_backward(inputs, labels_block, weights, totals, loss_scale):
    weight_one, bias_one, weight_two, bias_two = weights
    hidden_pre, hidden_act, logits = expert_forward(
        inputs, weight_one, bias_one, weight_two, bias_two
    )
    num_classes = logits.shape[1]
    probs = jax.nn.sigmoid(logits.astype(jnp.float32))
    classes = lax.broadcasted_iota(jnp.int32, (1, num_classes, 1), 1)
    onehot = (labels_block[:, None, :] == classes).astype(jnp.float32)
    live = (labels_block >= 0).astype(jnp.float32)[:, None, :]
    denom = (totals[1] + totals[2] + 1.0)[None, :, None]
    dice = (2.0 * totals[0] + 1.0)[None, :, None] / denom
    grad_prob = -loss_scale / num_classes * (2.0 * onehot - dice) / denom * live
    grad_logit = (grad_prob * probs * (1.0 - probs)).astype(jnp.bfloat16)
    grad_two = jnp.einsum(
        "bkn,bhn->bkh", grad_logit, hidden_act, preferred_element_type=jnp.float32
    )
    grad_bias_two = jnp.sum(grad_logit.astype(jnp.float32), axis=2)
    grad_hidden = jnp.einsum(
        "bkh,bkn->bhn", weight_two, grad_logit, preferred_element_type=jnp.float32
    ) * silu_grad(hidden_pre)
    grad_hidden = grad_hidden.astype(jnp.bfloat16)
    grad_one = jnp.einsum("bhn,bcn->bhc", grad_hidden, inputs, preferred_element_type=jnp.float32)
    grad_bias_one = jnp.sum(grad_hidden.astype(jnp.float32), axis=2)
    grad_inputs = jnp.einsum(
        "bhc,bhn->bcn", weight_one, grad_hidden, preferred_element_type=jnp.float32
    ).astype(jnp.bfloat16)
    return (grad_inputs, (grad_one, grad_bias_one, grad_two, grad_bias_two))


def on_device(
    features, kernel, labels, region_ids, first_weight, first_bias, second_weight, second_bias
):
    channels, depth_cells, height_cells, width_cells = features.shape
    classes = second_weight.shape[1]
    hidden_units = first_weight.shape[1]
    experts = lax.axis_size("expert")
    row_total = depth_cells * height_cells
    capacity = row_total // 8
    voxels = depth_cells * lax.axis_size("slab") * height_cells * experts * width_cells
    loss_scale = 16.0 * classes * math.sqrt(voxels)
    padded = with_halo(features, (("slab", 1), ("expert", 2)), 1)
    padded = jnp.pad(padded, ((0, 0), (0, 0), (0, 0), (1, 1)))
    conv_pre = jnp.zeros((channels, depth_cells, height_cells, width_cells), jnp.float32)
    for tap_index in range(27):
        conv_pre = conv_pre + jnp.einsum(
            "oc,czhw->ozhw",
            kernel[tap_index],
            shifted(padded, tap_index, depth_cells, height_cells, width_cells),
            preferred_element_type=jnp.float32,
        )
    conv_act = jax.nn.silu(conv_pre).astype(jnp.bfloat16)
    row_ids = region_ids.reshape(row_total)
    row_labels = labels.reshape(row_total, width_cells)
    zero_stats = jnp.zeros((3, classes), jnp.float32)
    expert_hot = (row_ids[:, None] == lax.broadcasted_iota(jnp.int32, (1, experts), 1)).astype(
        jnp.int32
    )
    earlier = jnp.cumsum(expert_hot, axis=0) - expert_hot
    position = jnp.sum(earlier * expert_hot, axis=1)
    slot_index = row_ids * capacity + position
    placing = lax.broadcasted_iota(jnp.int32, (experts * capacity, 1), 0) == slot_index[None, :]
    placing_b = placing.astype(jnp.bfloat16)
    row_major = conv_act.reshape(channels, row_total, width_cells)
    send_rows = (
        jnp.einsum("sr,crw->csw", placing_b, row_major, preferred_element_type=jnp.float32)
        .astype(jnp.bfloat16)
        .reshape(channels, experts, capacity, width_cells)
    )
    label_plus = (row_labels + 1).astype(jnp.float32)
    send_labels = (
        (jnp.dot(placing.astype(jnp.float32), label_plus, precision=lax.Precision.HIGHEST) - 1.0)
        .astype(jnp.bfloat16)
        .reshape(1, experts, capacity, width_cells)
    )
    got_rows, got_labels = (
        lax.all_to_all(send_rows, "expert", split_axis=1, concat_axis=1, tiled=True),
        lax.all_to_all(send_labels, "expert", split_axis=1, concat_axis=1, tiled=True),
    )
    block_inputs = jnp.transpose(got_rows, (1, 0, 2, 3)).reshape(
        experts, 1, channels, capacity * width_cells
    )
    block_labels = got_labels.astype(jnp.int32).reshape(experts, 1, capacity * width_cells)
    own_weights = (first_weight, first_bias, second_weight, second_bias)

    def first_pass(totals, pieces):
        inputs, labels_block = pieces
        logits = expert_forward(inputs, *own_weights)[2]
        return (totals + class_sums(logits, labels_block), None)

    partial_value, _ = lax.scan(first_pass, zero_stats, (block_inputs, block_labels))
    totals = lax.psum(partial_value, ("slab", "expert"))
    zero_grads = (
        jnp.zeros((1, hidden_units, channels), jnp.float32),
        jnp.zeros((1, hidden_units), jnp.float32),
        jnp.zeros((1, classes, hidden_units), jnp.float32),
        jnp.zeros((1, classes), jnp.float32),
    )

    def second_pass(grad_sums, pieces):
        inputs, labels_block = pieces
        grad_inputs, batch_grads = expert_backward(
            inputs, labels_block, own_weights, totals, loss_scale
        )
        return (tuple((total + piece for total, piece in zip(grad_sums, batch_grads))), grad_inputs)

    local_grads, grad_blocks = lax.scan(second_pass, zero_grads, (block_inputs, block_labels))
    backward_rows = jnp.transpose(
        grad_blocks.reshape(experts, channels, capacity, width_cells), (1, 0, 2, 3)
    )
    returned = lax.all_to_all(backward_rows, "expert", split_axis=1, concat_axis=1, tiled=True)
    grad_act = jnp.einsum(
        "sr,csw->crw",
        placing_b,
        returned.reshape(channels, experts * capacity, width_cells),
        preferred_element_type=jnp.float32,
    )
    expert_grads = lax.psum(
        (local_grads[0], local_grads[1], local_grads[2], local_grads[3]), "slab"
    )
    grad_pre = (
        grad_act.reshape(channels, depth_cells, height_cells, width_cells) * silu_grad(conv_pre)
    ).astype(jnp.bfloat16)
    local_kernel = jnp.stack(
        [
            jnp.einsum(
                "ozhw,czhw->oc",
                grad_pre,
                shifted(padded, tap_index, depth_cells, height_cells, width_cells),
                preferred_element_type=jnp.float32,
            )
            for tap_index in range(27)
        ]
    )
    grad_kernel = lax.psum(local_kernel, ("slab", "expert"))
    denom = totals[1] + totals[2] + 1.0
    dice = (2.0 * totals[0] + 1.0) / denom
    loss = 1.0 - jnp.mean(dice)
    return (loss, grad_kernel, expert_grads[0], expert_grads[1], expert_grads[2], expert_grads[3])


def solution(mesh):
    in_specs = (
        P(None, "slab", "expert", None),
        P(),
        P("slab", "expert", None),
        P("slab", "expert", None, None),
        P("expert", None, None),
        P("expert", None),
        P("expert", None, None),
        P("expert", None),
    )
    out_specs = (
        P(),
        P(),
        P("expert", None, None),
        P("expert", None),
        P("expert", None, None),
        P("expert", None),
    )
    return jax.shard_map(
        on_device, mesh=mesh, in_specs=in_specs, out_specs=out_specs, check_vma=False
    )
```

profile of v0, /device:TPU:1, one launch (start us, length us, event | category | flops | bytes accessed | tf_op | source)
XLA Modules:
  0.0 555.5 jit_solution(8662449189564305339)
XLA Ops:
  7.2 1.0 copy.150
  8.2 3.9 collective-permute-start
  12.2 1.3 collective-permute-start.1
  15.7 1.6 fusion.93
  17.3 9.4 %all-to-all-start = ((bf16[1,16,2,128]{3,2,0,1:T(2,128)(2,1)}), bf16[1,16,2,128]{3,2,0,1:T(2,128)(2,1)S(1)}, u32[]{:S(2)}, u32[]{:S(2)}) async-start(bf16[1,16,2,128]{3,2,0,1:T(2,128)(2,1)} %bitcast.3), calls=%async_computation | async-start | bytes 16384 | tf_op jit(solution)/shard_map/all_to_all | solution.py:143
  27.7 3.5 collective-permute-start.2
  31.3 2.1 collective-permute-start.3
  33.4 3.3 collective-permute-done.3
  42.5 1.0 copy.157
  43.5 7.2 %all-to-all-start.1 = ((bf16[32,16,2,128]{3,2,0,1:T(2,128)(2,1)}), bf16[32,16,2,128]{3,2,0,1:T(2,128)(2,1)S(1)}, u32[]{:S(2)}, u32[]{:S(2)}) async-start(bf16[32,16,2,128]{3,2,0,1:T(2,128)(2,1)} %copy.157), calls=%async_computation.1 | async-start | bytes 524288 | tf_op jit(solution)/shard_map/all_to_all | solution.py:142
  50.8 11.6 %all-to-all-done.1 = bf16[32,16,2,128]{3,2,0,1:T(2,128)(2,1)S(1)} async-done(((bf16[32,16,2,128]{3,2,0,1:T(2,128)(2,1)}), bf16[32,16,2,128]{3,2,0,1:T(2,128)(2,1)S(1)}, u32[]{:S(2)}, u32[]{:S(2)}) %all-to-all-start.1) | async-done | bytes 262176 | tf_op jit(solution)/shard_map/all_to_all | solution.py:142
  62.7 24.6 %while.32 = (s32[]{:T(128)}, f32[3,117]{1,0:T(4,128)S(1)}, s32[16,1,256]{2,1,0:T(1,128)S(1)}, bf16[16,1,32,256]{3,2,1,0:T(8,128)(2,1)S(1)}, bf16[1,256,32]{1,2,0...) while((s32[]{:T(128)}, f32[3,117]{1,0:T(4,128)S(1)}, ...), condition=%wide.region_6.7_spmd.clone, body=%wide.region_2.6_spmd.clone.sunk | while | flops 20344212 | bytes 109861 | solution.py:156
  64.8 0.9 fusion.290
  70.9 0.9 fusion.290
  75.5 0.9 fusion.290
  87.3 77.1 %psum.42 = f32[3,117]{1,0:T(4,128)S(1)} all-reduce(f32[3,117]{1,0:T(4,128)S(1)} %get-tuple-element.208), channel_id=1, replica_groups=mesh['slab'=16,'expert'=16] {'slab','expert'}, use_global_device_ids=true, to_apply=%region_7.8 | all-reduce | flops 351 | bytes 2808 | tf_op jit(solution)/shard_map/psum | solution.py:157
  165.0 24.0 %while.33 = (s32[]{:T(128)}, f32[1,256,32]{1,2,0:T(8,128)S(1)}, f32[1,256]{1,0:T(1,128)S(1)}, f32[1,117,256]{2,1,0:T(8,128)S(1)}, f32[1,117]{1,0:T(1,128)S(1)}, ...) while((s32[]{:T(128)}, f32[1,256,32]{1,2,0:T(8,128)S(1)}, ...), condition=%wide.region_12.13_spmd.clone, body=%wide.region_9.12_spmd.clone.sunk | while | flops 60328752 | bytes 2015584 | solution.py:172
  189.8 4.6 all-to-all-start.2
  194.4 1.6 fusion.254
  196.8 9.2 %all-to-all-done.2 = bf16[32,16,2,128]{3,2,0,1:T(2,128)(2,1)S(1)} async-done(((bf16[32,16,2,128]{3,2,0,1:T(2,128)(2,1)}), bf16[32,16,2,128]{3,2,0,1:T(2,128)(2,1)S(1)}, u32[]{:S(2)}, u32[]{:S(2)}) %all-to-all-start.2) | async-done | bytes 262176 | tf_op jit(solution)/shard_map/all_to_all | solution.py:176
  214.2 57.9 %all-reduce.1 = (f32[1,256,32]{1,2,0:T(8,128)}, f32[1,256]{1,0:T(1,128)}, f32[1,117]{1,0:T(1,128)}) all-reduce(f32[1,256,32]{1,2,0:T(8,128)S(1)} %get-tuple-element.210, f32[1,256]{1,0:T(1,128)S(1)} %get-tuple-element.211, f32[1,117]{1,0:T(1,128)S(1)} %get-tuple-element.213), channel_id=1, replica_groups=mesh['slab'=16,'expert'=16] {'slab'}, use_global_device_ids=true, to_apply=%region_14.15 | all-reduce | flops 8565 | bytes 68520 | tf_op jit(solution)/shard_map/psum | solution.py:183
  272.0 16.0 %all-reduce.7.cloned.1.call-done = f32[1,117,256]{2,0,1:T(1,128)} async-done(((f32[1,117,256]{2,0,1:T(1,128)}), f32[1,117,256]{2,0,1:T(1,128)}) %all-reduce.7.cloned.1.call-update) | async-done | bytes 119824 | tf_op jit(solution)/shard_map/psum | solution.py:183
  288.1 257.0 %all-reduce.5.cloned.1.call-done = f32[27,32,32]{2,1,0:T(8,128)} async-done(((f32[27,32,32]{2,1,0:T(8,128)}), f32[27,32,32]{2,1,0:T(8,128)}) %all-reduce.5.cloned.1.call-update) | async-done | bytes 110608 | tf_op jit(solution)/shard_map/psum | solution.py:200
  545.1 1.8 copy.441
  (430 shorter events, 63.3 us)
Async XLA Ops:
  7.2 19.6 %copy-start = (bf16[32,2,8,128]{3,2,1,0:T(8,128)(2,1)S(1)}, bf16[32,2,8,128]{3,2,1,0:T(8,128)(2,1)}, u32[]{:S(2)}) copy-start(bf16[32,2,8,128]{3,2,1,0:T(8,128)(2,1)} %param.12) | copy-start | bytes 393220
  8.2 19.4 %collective-permute-start = (bf16[32,1,8,128]{3,0,2,1:T(8,128)(2,1)S(1)}, bf16[32,1,8,128]{3,0,2,1:T(8,128)(2,1)S(1)}, u32[]{:S(2)}, u32[]{:S(2)}) collective-permute-start(bf16[32,1,8,128]{3,0,2,1:T(8,128)(2,1)S(1)} %get-tuple-element.421), channel_id=1, source_target_pairs={{0,16},{16,32},{32,48},{48,64},{64,80},{80,96},{96,112},{112,128},... | collective-permute-start | bytes 196616 | tf_op jit(solution)/shard_map/ppermute | solution.py:16
  12.2 15.5 %collective-permute-start.1 = (bf16[32,1,8,128]{3,0,2,1:T(8,128)(2,1)S(1)}, bf16[32,1,8,128]{3,0,2,1:T(8,128)(2,1)S(1)}, u32[]{:S(2)}, u32[]{:S(2)}) collective-permute-start(bf16[32,1,8,128]{3,0,2,1:T(8,128)(2,1)S(1)} %get-tuple-element.420), channel_id=1, source_target_pairs={{16,0},{32,16},{48,32},{64,48},{80,64},{96,80},{112,96},{128,112},... | collective-permute-start | bytes 196616 | tf_op jit(solution)/shard_map/ppermute | solution.py:17
  17.3 26.2 %all-to-all-start = ((bf16[1,16,2,128]{3,2,0,1:T(2,128)(2,1)}), bf16[1,16,2,128]{3,2,0,1:T(2,128)(2,1)S(1)}, u32[]{:S(2)}, u32[]{:S(2)}) async-start(bf16[1,16,2,128]{3,2,0,1:T(2,128)(2,1)} %bitcast.3), calls=%async_computation | async-start | bytes 16384 | tf_op jit(solution)/shard_map/all_to_all | solution.py:143
  27.7 5.7 %collective-permute-start.2 = (bf16[32,4,1,128]{3,0,2,1:T(8,128)(2,1)S(1)}, bf16[32,4,1,128]{3,0,2,1:T(8,128)(2,1)S(1)}, u32[]{:S(2)}, u32[]{:S(2)}) collective-permute-start(bf16[32,4,1,128]{3,0,2,1:T(8,128)(2,1)S(1)} %get-tuple-element.416), channel_id=1, source_target_pairs={{0,1},{1,2},{2,3},{3,4},{4,5},{5,6},{6,7},{7,8},{8,9},{9,10},{10,1... | collective-permute-start | bytes 98312 | tf_op jit(solution)/shard_map/ppermute | solution.py:16
  31.3 5.7 %copy-start.3 = (bf16[27,32,32]{2,1,0:T(8,128)(2,1)S(1)}, bf16[27,32,32]{2,1,0:T(8,128)(2,1)}, u32[]{:S(2)}) copy-start(bf16[27,32,32]{2,1,0:T(8,128)(2,1)} %param.13) | copy-start | bytes 165892
  31.3 5.4 collective-permute-start.3
  43.5 19.1 %copy-start.2 = (bf16[1,256,32]{1,2,0:T(8,128)(2,1)S(1)}, bf16[1,256,32]{1,2,0:T(8,128)(2,1)}, u32[]{:S(2)}) copy-start(bf16[1,256,32]{1,2,0:T(8,128)(2,1)} %param.16) | copy-start | bytes 49156
  43.5 19.1 %copy-start.16 = (bf16[1,256]{1,0:T(2,128)(2,1)S(1)}, bf16[1,256]{1,0:T(2,128)(2,1)}, u32[]{:S(2)}) copy-start(bf16[1,256]{1,0:T(2,128)(2,1)} %param.17) | copy-start | bytes 1540
  43.5 19.2 %copy-start.17 = (bf16[1,117,256]{2,1,0:T(8,128)(2,1)S(1)}, bf16[1,117,256]{2,1,0:T(8,128)(2,1)}, u32[]{:S(2)}) copy-start(bf16[1,117,256]{2,1,0:T(8,128)(2,1)} %param.18) | copy-start | bytes 179716
  43.5 19.2 %copy-start.18 = (bf16[1,117]{1,0:T(2,128)(2,1)S(1)}, bf16[1,117]{1,0:T(2,128)(2,1)}, u32[]{:S(2)}) copy-start(bf16[1,117]{1,0:T(2,128)(2,1)} %param.19) | copy-start | bytes 706
  43.5 18.9 %all-to-all-start.1 = ((bf16[32,16,2,128]{3,2,0,1:T(2,128)(2,1)}), bf16[32,16,2,128]{3,2,0,1:T(2,128)(2,1)S(1)}, u32[]{:S(2)}, u32[]{:S(2)}) async-start(bf16[32,16,2,128]{3,2,0,1:T(2,128)(2,1)} %copy.157), calls=%async_computation.1 | async-start | bytes 524288 | tf_op jit(solution)/shard_map/all_to_all | solution.py:142
  189.8 16.3 %all-to-all-start.2 = ((bf16[32,16,2,128]{3,2,0,1:T(2,128)(2,1)}), bf16[32,16,2,128]{3,2,0,1:T(2,128)(2,1)S(1)}, u32[]{:S(2)}, u32[]{:S(2)}) async-start(bf16[32,16,2,128]{3,2,0,1:T(2,128)(2,1)} %bitcast.109), calls=%async_computation.2 | async-start | bytes 524288 | tf_op jit(solution)/shard_map/all_to_all | solution.py:176
  194.3 93.7 %all-reduce.7.cloned.1.call-start = ((), (), s32[]{:S(2)}) async-start(), calls=%async_computation.4 | async-start | bytes 239616 | tf_op jit(solution)/shard_map/psum | solution.py:183
  196.8 348.3 %all-reduce.5.cloned.1.call-start = ((), (), s32[]{:S(2)}) async-start(), calls=%async_computation.3 | async-start | bytes 884736 | tf_op jit(solution)/shard_map/psum | solution.py:200
  206.6 1.1 copy-start.13
  206.7 1.2 copy-start.12
  207.5 0.9 copy-start.11
  207.7 0.9 copy-start.10
  208.0 1.0 copy-start.9
  208.8 1.0 copy-start.7
  209.5 1.0 copy-start.5
  209.7 0.9 copy-start.4
  288.1 258.9 %copy-start.15 = (f32[1,117,256]{2,0,1:T(1,128)S(1)}, f32[1,117,256]{2,0,1:T(1,128)}, u32[]{:S(2)}) copy-start(f32[1,117,256]{2,0,1:T(1,128)} %all-reduce.7.cloned.1.call-done) | copy-start | bytes 359428
  (4 other events, 3.6 us)
Sparse Core Ops, SparseCore 0:
  199.0 89.0 all-reduce.6
  295.1 249.9 all-reduce.4
where the time goes:
time: 556 us
  waiting for transfers between devices  297 us (53%)
  blocking collectives  135 us (24%)
  matrix products  42.4 us (8%)
  starting transfers between devices  32.1 us (6%)
  other arithmetic  20 us (4%)
  between operations  16.4 us (3%)
  local copies, waits for them, and re-layouts  10.5 us (2%)
    psum x1, waiting for transfers between devices, on_device(): grad_kernel = lax.psum(local_kernel, ('slab', 'expert'))  257 us
    psum x1, blocking collectives, on_device(): totals = lax.psum(partial_value, ('slab', 'expert'))  77.1 us
    psum x1, blocking collectives, on_device(): lax.psum((local_grads[0], local_grads[1], local_grads[2], local_grads[3])...  57.9 us
    psum x1, waiting for transfers between devices, on_device(): lax.psum((local_grads[0], local_grads[1], local_grads[2], local_grads[3])...  16 us
    reduce_sum x16, other arithmetic, class_sums(): jnp.sum(onehot, axis=(0, 2))  15.2 us
    dot_general x32, matrix products, expert_forward(): jnp.einsum('bkh,bhn->bkn', weight_two, hidden_act, preferred_element_type...  13.4 us
    all_to_all x1, waiting for transfers between devices, on_device(): lax.all_to_all(send_rows, 'expert', split_axis=1, concat_axis=1, tiled=True)  11.6 us
  transfers between devices with their start and end apart: 9, of which 5 were waited for; matrix products, arithmetic and copies ran while one was open for 3% of the time, Pallas kernels for 0%

commit v1 on v0

v1 whole, which is shorter than its diff:
```python
import functools
import math

import jax
import jax.numpy as jnp
from jax import lax
from jax.experimental import pallas as pl
from jax.experimental.pallas import tpu as pltpu
from jax.sharding import PartitionSpec as P

MESH = pl.DeviceIdType.MESH
BF16 = jnp.bfloat16
F32 = jnp.float32
I32 = jnp.int32
C = 32
W = 128
HID = 256
NCLS = 117
CLS = 128
ROWS = 16
CAP = 2
BLK = CAP * W
TAPS = 9
GROWS = 16

NT = (((1,), (1,)), ((), ()))
NN = (((1,), (0,)), ((), ()))

HALO = tuple((ds, de) for ds in (-1, 0, 1) for de in (-1, 0, 1) if (ds, de) != (0, 0))


def dot(a, b, dims=NN):
    return lax.dot_general(a, b, dims, preferred_element_type=F32)


def send_part(step, whole):
    return {1: pl.ds(whole, 1), -1: pl.ds(1, 1), 0: pl.ds(1, whole)}[step]


def land_part(step, whole):
    return {1: pl.ds(0, 1), -1: pl.ds(whole + 1, 1), 0: pl.ds(1, whole)}[step]


def body(
    ns, ne,
    x_hbm, k_hbm, lab_hbm, ids_hbm, w1_hbm, b1_hbm, w2_hbm, b2_hbm,
    loss_out, eg_out, gkc_out,
    x_ref, k_ref, lab_ref, ids_ref, w1_ref, b1_ref, w2_ref, b2_ref, in_sem,
    loss_ref, out_sem,
    xf, xp, kwf, kw, x9, act, dconv, lab_ext, lab_snd, lab_rcv, inv,
    w1a, w1t, w2f, w2h, w2t, b2bc, row_snd, row_rcv, xa_all, ha_all, d_all, q_all,
    acc_i, acc_m, acc_c, st1, st2, ab_b, b_b, gl_all, gh_all, ret_snd, ret_rcv, acc_g,
    egf, eg_snd, eg_rcv, eg_all, gp3, gka_snd, gka_rcv, gkb, gkc,
    halo_s, halo_r, lab_s, lab_r, row_s, row_r, st1_s, st1_r, st2_s, st2_r,
    ret_s, ret_r, eg_s, eg_r, ega_s, ega_r, gka_s, gka_r, gkb_s, gkb_r, gkc_s, gkc_r,
):
    me_s = lax.axis_index("slab")
    me_e = lax.axis_index("expert")

    def remote(src, dst, ssem, rsem, s, e):
        return pltpu.make_async_remote_copy(
            src_ref=src, dst_ref=dst, send_sem=ssem, recv_sem=rsem,
            device_id=(s, e), device_id_type=MESH,
        )

    def loop(lo, hi, fn):
        def step(i, carry):
            fn(i)
            return carry
        lax.fori_loop(lo, hi, step, 0)

    def epeer(k):
        return lax.rem(me_e + k, ne)

    def speer(k):
        return lax.rem(me_s + k, ns)

    def exists(ds, de):
        ok = None
        for step, me, n in ((ds, me_s, ns), (de, me_e, ne)):
            if step:
                cond = (me < n - 1) if step > 0 else (me > 0)
                ok = cond if ok is None else jnp.logical_and(ok, cond)
        return ok

    drains = []
    pairs = (
        (x_hbm, x_ref), (ids_hbm, ids_ref), (lab_hbm, lab_ref), (k_hbm, k_ref),
        (w1_hbm, w1_ref), (b1_hbm, b1_ref), (w2_hbm, w2_ref), (b2_hbm, b2_ref),
    )
    loads = [pltpu.make_async_copy(src, dst, in_sem.at[i]) for i, (src, dst) in enumerate(pairs)]
    for load in loads:
        load.start()

    results = ((loss_ref, loss_out), (eg_all, eg_out), (gkc, gkc_out))
    stores = [pltpu.make_async_copy(src, dst, out_sem.at[i]) for i, (src, dst) in enumerate(results)]

    zrow = jnp.zeros((10, C, W), BF16)
    xp[0] = zrow
    xp[3] = zrow
    for z in (1, 2):
        for h in (0, 9):
            xp[z, h] = jnp.zeros((C, W), BF16)

    barrier = pltpu.get_barrier_semaphore()
    loop(1, ne, lambda k: pl.semaphore_signal(barrier, 1, device_id=(me_s, epeer(k)), device_id_type=MESH))
    loop(1, ns, lambda k: pl.semaphore_signal(barrier, 1, device_id=(speer(k), me_e), device_id_type=MESH))
    for ds, de in HALO:
        if ds and de:
            @pl.when(exists(ds, de))
            def _():
                pl.semaphore_signal(barrier, 1, device_id=(me_s + ds, me_e + de), device_id_type=MESH)
    n_s = (me_s > 0).astype(I32) + (me_s < ns - 1).astype(I32)
    n_e = (me_e > 0).astype(I32) + (me_e < ne - 1).astype(I32)

    loads[0].wait()

    xf[...] = x_ref[...].astype(F32)
    for r in range(ROWS):
        xp[1 + r // 8, 1 + r % 8] = xf[pl.ds(r, C, stride=ROWS), :].astype(BF16)

    pl.semaphore_wait(barrier, (ne - 1) + (ns - 1) + n_s * n_e)

    def halo_copy(d, s, e):
        ds, de = HALO[d]
        return remote(
            xp.at[send_part(ds, 2), send_part(de, 8)],
            xp.at[land_part(ds, 2), land_part(de, 8)],
            halo_s.at[d], halo_r.at[d], s, e,
        )

    for d, (ds, de) in enumerate(HALO):
        @pl.when(exists(ds, de))
        def _():
            halo_copy(d, me_s + ds, me_e + de).start()

    loads[1].wait()
    loads[2].wait()

    ids = [ids_ref[r] for r in range(ROWS)]

    def place(e):
        first = jnp.int32(ROWS)
        second = jnp.int32(ROWS)
        for r in reversed(range(ROWS)):
            hit = ids[r] == e
            second = jnp.where(hit, first, second)
            first = jnp.where(hit, jnp.int32(r), first)
        inv[2 * e] = first
        inv[2 * e + 1] = second

    loop(0, ne, place)
    lab_ext[0:ROWS, :] = lab_ref[...]
    lab_ext[ROWS:, :] = jnp.full((8, W), -1, I32)
    act[ROWS] = jnp.zeros((C, W), BF16)

    def put_labels(e):
        lab_snd[e, 0:1] = lab_ext[pl.ds(inv[2 * e], 1), :]
        lab_snd[e, 1:2] = lab_ext[pl.ds(inv[2 * e + 1], 1), :]

    loop(0, ne, put_labels)

    def lab_copy(at, e):
        return remote(lab_snd.at[e], lab_rcv.at[at], lab_s.at[e], lab_r.at[at], me_s, e)

    loop(1, ne, lambda k: lab_copy(me_e, epeer(k)).start())
    lab_rcv[pl.ds(me_e, 1)] = lab_snd[pl.ds(me_e, 1)]

    def drain_halo():
        for d, (ds, de) in enumerate(HALO):
            @pl.when(exists(ds, de))
            def _():
                halo_copy(d, me_s + ds, me_e + de).wait_send()

    drains.append(drain_halo)
    drains.append(lambda: loop(1, ne, lambda k: lab_copy(me_e, epeer(k)).wait_send()))

    for load in loads[3:]:
        load.wait()

    for tap in range(27):
        a, b, c = tap // 9, tap // 3 % 3, tap % 3
        kwf[c * C:(c + 1) * C, (a * 3 + b) * C:(a * 3 + b + 1) * C] = k_ref[tap].astype(F32) * 0.5
    kw[...] = kwf[...].astype(BF16)
    w1 = w1_ref[...].astype(F32) * 0.5
    b1 = b1_ref[...].astype(F32) * 0.5
    w1full = jnp.concatenate([w1, b1, jnp.zeros((CLS - C - 1, HID), F32)], axis=0)
    w1t[...] = w1.astype(BF16)
    w1a[...] = w1full.T.astype(BF16)
    w2f[...] = jnp.zeros((CLS, HID), F32)
    w2f[0:NCLS, :] = w2_ref[...].astype(F32) * 0.5
    w2h[...] = w2f[...].astype(BF16)
    w2t[...] = w2f[...].T.astype(BF16)
    acc_c[0:8, :] = jnp.zeros((8, CLS), F32)
    acc_c[0:1, 0:NCLS] = b2_ref[...].astype(F32) * 0.5
    b2bc[...] = jnp.broadcast_to(acc_c[0:1, :], (CLS, CLS)).T

    classes = lax.broadcasted_iota(I32, (CLS, W), 0)
    lanes = lax.broadcasted_iota(I32, (C, W), 1)
    acc_i[...] = jnp.zeros((CLS, W), F32)
    acc_m[...] = jnp.zeros((CLS, W), F32)
    acc_c[...] = jnp.zeros((CLS, W), F32)
    acc_g[...] = jnp.zeros((CLS, W), F32)

    def count(r):
        acc_c[...] += jnp.where(classes == lab_ext[pl.ds(r, 1), :], 1.0, 0.0)

    loop(0, ROWS, count)

    for d, (ds, de) in enumerate(HALO):
        @pl.when(exists(-ds, -de))
        def _():
            halo_copy(d, me_s - ds, me_e - de).wait_recv()

    def gather(z):
        for h in range(8):
            lane = slice((z * 8 + h) * W, (z * 8 + h + 1) * W)
            for a in range(3):
                x9[a * 96:(a + 1) * 96, lane] = xp[z + a, h:h + 3].reshape(96, W)

    for z in range(2):
        gather(z)

    def conv(p):
        lane = slice(p * BLK, (p + 1) * BLK)
        out = dot(kw[...], x9[:, lane])
        for j in range(2):
            part = out[:, j * W:(j + 1) * W]
            left = jnp.where(lanes > 0, pltpu.roll(part[0:C], 1, 1), 0.0)
            right = jnp.where(lanes < W - 1, pltpu.roll(part[2 * C:3 * C], W - 1, 1), 0.0)
            v = left + part[C:2 * C] + right
            t = jnp.tanh(v)
            act[2 * p + j] = (v + v * t).astype(BF16)
            dconv[2 * p + j] = (1.0 + t) + v * (1.0 - t * t)

    for p in range(ROWS // 2):
        conv(p)

    half = ne // 2

    def turn(i):
        m = (i + 1) // 2
        return half + m * (1 - 2 * lax.rem(i, 2))

    def row_copy(at, e):
        return remote(row_snd.at[e], row_rcv.at[at], row_s.at[e], row_r.at[at], me_s, e)

    def dispatch(i):
        e = epeer(turn(i))
        row_snd[e, 0] = act[inv[2 * e]]
        row_snd[e, 1] = act[inv[2 * e + 1]]
        row_copy(me_e, e).start()

    loop(0, ne - 1, dispatch)
    drains.append(lambda: loop(1, ne, lambda k: row_copy(me_e, epeer(k)).wait_send()))
    row_rcv[me_e, 0] = act[inv[2 * me_e]]
    row_rcv[me_e, 1] = act[inv[2 * me_e + 1]]

    ones = jnp.where(lax.broadcasted_iota(I32, (16, BLK), 0) == 0, 1.0, 0.0).astype(BF16)

    def forward(*blocks):
        ti = acc_i[...]
        tm = acc_m[...]
        for s in blocks:
            col = pl.ds(pl.multiple_of(s * BLK, BLK), BLK)
            x = row_rcv[s]
            xa = jnp.concatenate([jnp.concatenate([x[0], x[1]], axis=1), ones], axis=0)
            xa_all[:, col] = xa
            v = dot(w1a[:, 0:48], xa)
            t = jnp.tanh(v)
            ha = (v + v * t).astype(BF16)
            ha_all[:, col] = ha
            d_all[:, col] = (1.0 + t) + v * (1.0 - t * t)
            z = dot(w2h[...], ha)
            lab = lab_rcv[s]
            for j in range(CAP):
                lj = lab[j:j + 1, :]
                t2 = jnp.tanh(z[:, j * W:(j + 1) * W] + b2bc[...])
                t2 = jnp.where(lj < 0, 1.0, t2)
                q_all[:, pl.ds(pl.multiple_of(s * BLK + j * W, W), W)] = 1.0 - t2 * t2
                ti = ti + jnp.where(classes == lj, t2, 0.0)
                tm = tm + t2
        acc_i[...] = ti
        acc_m[...] = tm

    def arrived(s):
        lab_copy(s, s).wait_recv()
        row_copy(s, s).wait_recv()

    forward(me_e)

    def forward_turn(k):
        before, behind = epeer(ne - k), epeer(k)
        arrived(before)
        arrived(behind)
        forward(before, behind)

    loop(1, half, forward_turn)
    arrived(epeer(half))
    forward(epeer(half))

    def lane_row(m):
        return jnp.sum(m.T, axis=0, keepdims=True)

    st1[pl.ds(me_e, 1)] = jnp.concatenate(
        [lane_row(acc_i[...]), lane_row(acc_m[...]), lane_row(acc_c[...]), jnp.zeros((1, CLS), F32)],
        axis=0,
    )[None]

    def st1_copy(at, e, k):
        return remote(st1.at[at], st1.at[at], st1_s.at[k], st1_r.at[at], me_s, e)

    loop(1, ne, lambda k: st1_copy(me_e, epeer(k), k).start())
    drains.append(lambda: loop(1, ne, lambda k: st1_copy(me_e, epeer(k), k).wait_send()))
    loop(1, ne, lambda k: st1_copy(epeer(k), epeer(k), k).wait_recv())
    st2[pl.ds(me_s, 1)] = jnp.sum(st1[...], axis=0)[None]

    def st2_copy(at, s, k):
        return remote(st2.at[at], st2.at[at], st2_s.at[k], st2_r.at[at], s, me_e)

    loop(1, ns, lambda k: st2_copy(me_s, speer(k), k).start())
    drains.append(lambda: loop(1, ns, lambda k: st2_copy(me_s, speer(k), k).wait_send()))
    loop(1, ns, lambda k: st2_copy(speer(k), speer(k), k).wait_recv())
    sums = jnp.sum(st2[...], axis=0)

    voxels = ns * ne * ROWS * W
    slots = ns * ne * ne * BLK
    scale = 16.0 * NCLS * math.sqrt(voxels)
    cnt = sums[2:3]
    inter = 0.5 * (cnt + sums[0:1])
    mass = 0.5 * sums[1:2] + (voxels - 0.5 * slots)
    denom = mass + cnt + 1.0
    dice = (2.0 * inter + 1.0) / denom
    real = lax.broadcasted_iota(I32, (1, CLS), 1) < NCLS
    loss_ref[...] = 1.0 - jnp.sum(jnp.where(real, dice, 0.0), axis=1, keepdims=True) / NCLS
    coef = jnp.where(real, (0.25 * scale / NCLS) / denom, 0.0)
    ab_b[...] = jnp.broadcast_to(coef * (dice - 2.0), (CLS, CLS)).T
    b_b[...] = jnp.broadcast_to(coef * dice, (CLS, CLS)).T

    def backward(dst, *blocks):
        tg = acc_g[...]
        for s in blocks:
            col = pl.ds(pl.multiple_of(s * BLK, BLK), BLK)
            lab = lab_rcv[s]
            parts = []
            for j in range(CAP):
                eq = classes == lab[j:j + 1, :]
                g = jnp.where(eq, ab_b[...], b_b[...])
                g = g * q_all[:, pl.ds(pl.multiple_of(s * BLK + j * W, W), W)]
                tg = tg + g
                parts.append(g.astype(BF16))
            gl = jnp.concatenate(parts, axis=1)
            gl_all[:, col] = gl
            gh = (dot(w2t[...], gl) * d_all[:, col]).astype(BF16)
            gh_all[:, col] = gh
            gx = dot(w1t[...], gh).astype(BF16)
            dst[s, 0] = gx[:, 0:W]
            dst[s, 1] = gx[:, W:]
        acc_g[...] = tg

    def ret_copy(at, e):
        return remote(ret_snd.at[e], ret_rcv.at[at], ret_s.at[e], ret_r.at[at], me_s, e)

    def backward_turn(i):
        k = half - i
        before, behind = epeer(ne - k), epeer(k)
        backward(ret_snd, before, behind)
        ret_copy(me_e, before).start()
        ret_copy(me_e, behind).start()

    backward(ret_snd, epeer(half))
    ret_copy(me_e, epeer(half)).start()
    loop(1, half, backward_turn)
    drains.append(lambda: loop(1, ne, lambda k: ret_copy(me_e, epeer(k)).wait_send()))
    backward(ret_rcv, me_e)

    egf[:, 0:8, :] = dot(gl_all[...], ha_all[...], NT).reshape(GROWS, 8, HID)
    gw1 = dot(xa_all[...], gh_all[...], NT)
    for i in range(GROWS):
        egf[i, 8:10, :] = gw1[2 * i:2 * i + 2, :]
        egf[i, 10:11, :] = gw1[C:C + 1, :]
        egf[i, 11:16, :] = jnp.zeros((5, HID), F32)
    gb2 = lane_row(acc_g[...])
    egf[0, 11:12, 0:CLS] = gb2
    eg_snd[...] = egf[...].astype(BF16)
    own = GROWS // ns

    def eg_copy(at, s):
        return remote(eg_snd.at[pl.ds(s * own, own)], eg_rcv.at[at], eg_s.at[s], eg_r.at[at], s, me_e)

    loop(1, ns, lambda k: eg_copy(me_s, speer(k)).start())
    drains.append(lambda: loop(1, ns, lambda k: eg_copy(me_s, speer(k)).wait_send()))
    eg_rcv[pl.ds(me_s, 1)] = eg_snd[pl.ds(me_s * own, own)][None]

    loop(1, ne, lambda k: ret_copy(epeer(k), epeer(k)).wait_recv())
    gp3[96:, :] = jnp.zeros((CLS - 96, ROWS * W), BF16)

    def conv_back(r):
        lane = slice(r * W, (r + 1) * W)
        e = ids_ref[r]
        j = jnp.where(inv[2 * e] == r, 0, 1)
        gp = (ret_rcv[e, j].astype(F32) * dconv[r]).astype(BF16).astype(F32)
        gp3[0:C, lane] = jnp.where(lanes < W - 1, pltpu.roll(gp, W - 1, 1), 0.0).astype(BF16)
        gp3[C:2 * C, lane] = gp.astype(BF16)
        gp3[2 * C:3 * C, lane] = jnp.where(lanes > 0, pltpu.roll(gp, 1, 1), 0.0).astype(BF16)

    for r in range(ROWS):
        conv_back(r)
    gkt = dot(x9[...], gp3[...], NT)
    rest = jnp.concatenate([pltpu.roll(gkt[216:], 96 - c * C, 1) for c in range(3)], axis=0)
    full = jnp.where(lax.broadcasted_iota(I32, (216, CLS), 1) < 96, gkt[0:216], rest)
    full = jnp.concatenate([full, jnp.zeros((40, CLS), F32)], axis=0)
    gka_snd[...] = full.astype(BF16).reshape(GROWS, 16, CLS)

    def gka_copy(at, s):
        return remote(gka_snd.at[pl.ds(s * own, own)], gka_rcv.at[at], gka_s.at[s], gka_r.at[at], s, me_e)

    loop(1, ns, lambda k: gka_copy(me_s, speer(k)).start())
    drains.append(lambda: loop(1, ns, lambda k: gka_copy(me_s, speer(k)).wait_send()))
    gka_rcv[pl.ds(me_s, 1)] = gka_snd[pl.ds(me_s * own, own)][None]

    loop(1, ns, lambda k: eg_copy(speer(k), speer(k)).wait_recv())
    eg_all[pl.ds(me_s * own, own)] = jnp.sum(eg_rcv[...].astype(F32), axis=0).astype(BF16)

    def ega_copy(at, s, k):
        part = eg_all.at[pl.ds(at * own, own)]
        return remote(part, part, ega_s.at[k], ega_r.at[at], s, me_e)

    loop(1, ns, lambda k: ega_copy(me_s, speer(k), k).start())
    drains.append(lambda: loop(1, ns, lambda k: ega_copy(me_s, speer(k), k).wait_send()))

    loop(1, ns, lambda k: gka_copy(speer(k), speer(k)).wait_recv())
    gkb[pl.ds(me_e, 1)] = jnp.sum(gka_rcv[...].astype(F32), axis=0).astype(BF16)[None]

    def gkb_copy(at, e, k):
        return remote(gkb.at[at], gkb.at[at], gkb_s.at[k], gkb_r.at[at], me_s, e)

    loop(1, ne, lambda k: gkb_copy(me_e, epeer(k), k).start())
    drains.append(lambda: loop(1, ne, lambda k: gkb_copy(me_e, epeer(k), k).wait_send()))
    loop(1, ne, lambda k: gkb_copy(epeer(k), epeer(k), k).wait_recv())
    gkc[pl.ds(me_s * own, own)] = jnp.sum(gkb[...].astype(F32), axis=0).astype(BF16)

    def gkc_copy(at, s, k):
        part = gkc.at[pl.ds(at * own, own)]
        return remote(part, part, gkc_s.at[k], gkc_r.at[at], s, me_e)

    loop(1, ns, lambda k: gkc_copy(me_s, speer(k), k).start())
    drains.append(lambda: loop(1, ns, lambda k: gkc_copy(me_s, speer(k), k).wait_send()))
    loop(1, ns, lambda k: ega_copy(speer(k), speer(k), k).wait_recv())
    stores[0].start()
    stores[1].start()

    loop(1, ns, lambda k: gkc_copy(speer(k), speer(k), k).wait_recv())
    stores[2].start()
    for drain in drains:
        drain()
    for store in stores:
        store.wait()


def write_out(
    loss_in, eg_in, gkc_in, loss_out, gk_out, gw1_out, gb1_out, gw2_out, gb2_out,
    loss, eg, gkc, gk, gw1, gb1, gw2, gb2, isem, osem,
):
    pairs = ((gkc_in, gkc), (eg_in, eg), (loss_in, loss))
    loads = [pltpu.make_async_copy(src, dst, isem.at[i]) for i, (src, dst) in enumerate(pairs)]
    for load in loads:
        load.start()
    loads[0].wait()
    full = gkc[...].astype(F32).reshape(GROWS * 16, CLS)
    lanes = lax.broadcasted_iota(I32, (72, CLS), 1)
    rest = pltpu.roll(full[0:72], C, 1)
    for c in (1, 2):
        rest = jnp.where(lanes < c * C, rest, pltpu.roll(full[c * 72:(c + 1) * 72], (c + 1) * C, 1))
    gkt = jnp.concatenate([full[0:216], rest], axis=0)
    for j in range(TAPS):
        turned = gkt[j * C:(j + 1) * C]
        turned = jnp.concatenate([turned, jnp.zeros((CLS - C, CLS), F32)], axis=0).T
        for c in range(3):
            gk[3 * j + c] = turned[c * C:(c + 1) * C, 0:C]
    pairs = ((gk, gk_out), (gw1, gw1_out), (gb1, gb1_out), (gw2, gw2_out.at[:, 0, :]), (gb2, gb2_out), (loss, loss_out))
    stores = [pltpu.make_async_copy(src, dst, osem.at[i]) for i, (src, dst) in enumerate(pairs)]
    stores[0].start()
    loads[1].wait()
    loads[2].wait()
    stores[5].start()
    final = eg[...].astype(F32)
    gw2[...] = final[:, 0:8, :].reshape(CLS, HID)[0:NCLS]
    stores[3].start()
    for i in range(GROWS):
        gw1[2 * i:2 * i + 2, :] = final[i, 8:10, :]
    gb1[...] = final[0, 10:11, :]
    gb2[...] = final[0, 11:12, 0:NCLS]
    for i in (1, 2, 4):
        stores[i].start()
    for store in stores:
        store.wait()


def on_device(
    features, kernel, labels, region_ids, first_weight, first_bias, second_weight, second_bias
):
    ns, ne = lax.axis_size("slab"), lax.axis_size("expert")
    cols = ne * BLK
    V = pltpu.VMEM
    own = GROWS // ns
    scratch = [
        V((C * ROWS, W), BF16),
        V((27, C, C), BF16),
        V((ROWS, W), I32),
        pltpu.SMEM((ROWS,), I32),
        V((C, HID), BF16),
        V((1, HID), BF16),
        V((NCLS, HID), BF16),
        V((1, NCLS), BF16),
        pltpu.SemaphoreType.DMA((8,)),
        V((1, 1), F32),
        pltpu.SemaphoreType.DMA((3,)),
        V((C * ROWS, W), F32),
        V((4, 10, C, W), BF16),
        V((3 * C, TAPS * C), F32),
        V((3 * C, TAPS * C), BF16),
        V((TAPS * C, ROWS * W), BF16),
        V((ROWS + 1, C, W), BF16),
        V((ROWS, C, W), F32),
        V((ROWS + 8, W), I32),
        V((ne, CAP, W), I32),
        V((ne, CAP, W), I32),
        pltpu.SMEM((CAP * ne,), I32),
        V((HID, CLS), BF16),
        V((C, HID), BF16),
        V((CLS, HID), F32),
        V((CLS, HID), BF16),
        V((HID, CLS), BF16),
        V((CLS, W), F32),
        V((ne, CAP, C, W), BF16),
        V((ne, CAP, C, W), BF16),
        V((48, cols), BF16),
        V((HID, cols), BF16),
        V((HID, cols), F32),
        V((CLS, cols), F32),
        V((CLS, W), F32),
        V((CLS, W), F32),
        V((CLS, W), F32),
        V((ne, 4, CLS), F32),
        V((ns, 4, CLS), F32),
        V((CLS, W), F32),
        V((CLS, W), F32),
        V((CLS, cols), BF16),
        V((HID, cols), BF16),
        V((ne, CAP, C, W), BF16),
        V((ne, CAP, C, W), BF16),
        V((CLS, W), F32),
        V((GROWS, 16, HID), F32),
        V((GROWS, 16, HID), BF16),
        V((ns, own, 16, HID), BF16),
        V((GROWS, 16, HID), BF16),
        V((CLS, ROWS * W), BF16),
        V((GROWS, 16, CLS), BF16),
        V((ns, own, 16, CLS), BF16),
        V((ne, own, 16, CLS), BF16),
        V((GROWS, 16, CLS), BF16),
    ]
    sems = [8, 8, ne, ne, ne, ne, ne, ne, ns, ns, ne, ne, ns, ns, ns, ns, ns, ns, ne, ne, ns, ns]
    scratch += [pltpu.SemaphoreType.DMA((n,)) for n in sems]
    hbm = pl.BlockSpec(memory_space=pltpu.HBM)
    outs = pl.pallas_call(
        functools.partial(body, ns, ne),
        out_shape=[
            jax.ShapeDtypeStruct((1, 1), F32),
            jax.ShapeDtypeStruct((GROWS, 16, HID), BF16),
            jax.ShapeDtypeStruct((GROWS, 16, CLS), BF16),
        ],
        in_specs=[hbm] * 8,
        out_specs=[hbm] * 3,
        scratch_shapes=scratch,
        compiler_params=pltpu.CompilerParams(
            collective_id=0, has_side_effects=True, vmem_limit_bytes=63 * 2**20
        ),
        name="fused_head",
    )(
        features.reshape(C * ROWS, W),
        kernel,
        labels.reshape(ROWS, W),
        region_ids.reshape(ROWS),
        jnp.swapaxes(first_weight, 1, 2).reshape(C, HID),
        first_bias,
        second_weight.reshape(NCLS, HID),
        second_bias,
    )
    loss, gk, gw1, gb1, gw2, gb2 = pl.pallas_call(
        write_out,
        out_shape=[
            jax.ShapeDtypeStruct((1, 1), F32),
            jax.ShapeDtypeStruct((27, C, C), F32),
            jax.ShapeDtypeStruct((C, HID), F32),
            jax.ShapeDtypeStruct((1, HID), F32),
            jax.ShapeDtypeStruct((NCLS, 1, HID), F32),
            jax.ShapeDtypeStruct((1, NCLS), F32),
        ],
        in_specs=[hbm] * 3,
        out_specs=[hbm] * 6,
        scratch_shapes=[
            V((1, 1), F32),
            V((GROWS, 16, HID), BF16),
            V((GROWS, 16, CLS), BF16),
            V((27, C, C), F32),
            V((C, HID), F32),
            V((1, HID), F32),
            V((NCLS, HID), F32),
            V((1, NCLS), F32),
            pltpu.SemaphoreType.DMA((3,)),
            pltpu.SemaphoreType.DMA((6,)),
        ],
        name="write_out",
    )(*outs)
    return (
        loss.reshape(()),
        gk,
        jnp.swapaxes(gw1.reshape(1, C, HID), 1, 2),
        gb1,
        jnp.swapaxes(gw2, 0, 1),
        gb2,
    )


def solution(mesh):
    in_specs = (
        P(None, "slab", "expert", None),
        P(),
        P("slab", "expert", None),
        P("slab", "expert", None, None),
        P("expert", None, None),
        P("expert", None),
        P("expert", None, None),
        P("expert", None),
    )
    out_specs = (
        P(),
        P(),
        P("expert", None, None),
        P("expert", None),
        P("expert", None, None),
        P("expert", None),
    )
    return jax.shard_map(
        on_device, mesh=mesh, in_specs=in_specs, out_specs=out_specs, check_vma=False
    )
```

time: 556 us -> 68.6 us (0.12)
  waiting for transfers between devices: 297 us -> 0 us
  blocking collectives: 135 us -> 0 us
  Pallas kernels: 0 us -> 67.9 us
  matrix products: 42.4 us -> 0 us
  starting transfers between devices: 32.1 us -> 0 us
  other arithmetic: 20 us -> 0 us
  between operations: 16.4 us -> 0.64 us
  local copies, waits for them, and re-layouts: 10.5 us -> 0 us
    psum x2 -> x0, waiting for transfers between devices: 273 us -> none  [the longest x1 257 us: on_device(): grad_kernel = lax.psum(local_kernel, ('slab', 'expert'))]
    psum x2 -> x0, blocking collectives: 135 us -> none  [the longest x1 77.1 us: on_device(): totals = lax.psum(partial_value, ('slab', 'expert'))]
    pallas_call x0 -> x2, Pallas kernels: none -> 67.9 us  [the longest x1 65.4 us: on_device(): pl.pallas_call(functools.partial(body, ns, ne), out_shape=[jax.ShapeDtype...]
    dot_general x169 -> x0, matrix products: 42.4 us -> none  [the longest x32 13.4 us: expert_forward(): jnp.einsum('bkh,bhn->bkn', weight_two, hidden_act, preferred_element_type...]
    all_to_all x3 -> x0, starting transfers between devices: 21.2 us -> none  [the longest x1 9.43 us: on_device(): lax.all_to_all(send_labels, 'expert', split_axis=1, concat_axis=1, tiled=...]
    all_to_all x3 -> x0, waiting for transfers between devices: 20.8 us -> none  [the longest x1 11.6 us: on_device(): lax.all_to_all(send_rows, 'expert', split_axis=1, concat_axis=1, tiled=True)]
    reduce_sum x17 -> x0, other arithmetic: 16 us -> none  [the longest x16 15.2 us: class_sums(): jnp.sum(onehot, axis=(0, 2))]
    ppermute x4 -> x0, starting transfers between devices: 10.8 us -> none  [the longest x2 7.49 us: with_halo(): before = lax.ppermute(last, axis, up)]
  transfers between devices with their start and end apart: 9 -> 0, of which waited for: 5 -> 0; matrix products, arithmetic and copies ran while one was open for 3% -> 0% of each run, Pallas kernels for 0% -> 0%
where the time goes in v1:
time: 68.6 us; the launch traced here: 68.5 us
  Pallas kernels  67.9 us (99%)
    pallas_call x1, Pallas kernels, on_device(): pl.pallas_call(functools.partial(body, ns, ne), out_shape=[jax.ShapeDtype...  65.4 us
    pallas_call x1, Pallas kernels, on_device(): pl.pallas_call(write_out, out_shape=[jax.ShapeDtypeStruct((1, 1), F32), j...  2.47 us

profile of v1, /device:TPU:1, one launch (start us, length us, event | category | flops | bytes accessed | tf_op | source)
XLA Modules:
  0.0 68.5 jit_solution(4813716764018555627)
XLA Ops:
  0.6 65.4 %fused_head.1 = (f32[1,1]{1,0:T(1,128)}, bf16[16,16,256]{2,1,0:T(8,128)(2,1)}, bf16[16,16,128]{2,1,0:T(8,128)(2,1)}) custom-call(bf16[512,128]{1,0:T(8,128)(2,1)} %bitcast.12, bf16[27,32,32]{2,1,0:T(8,128)(2,1)} %k_hbm.1, s32[16,128]{1,0:T(8,128)} %bitcast.15, s32[16]{0:T(128)} %bitcast.16, bf16[32,256]{1,0:T(8,128)(2,1)} %bitcast.14, ...), custom_call_target="tpu_custom_call" | custom-call | tf_op jit(solution)/shard_map/fused_head/pallas_call | solution.py:567
  66.1 2.5 %write_out.1 = (f32[1,1]{1,0:T(1,128)}, f32[27,32,32]{2,1,0:T(8,128)}, f32[32,256]{1,0:T(8,128)}, f32[1,256]{1,0:T(1,128)}, f32[117,1,256]{2,1,0:T(1,128)}, /*index=5*/f32[1,117]{1,0:T(1,128)}) custom-call(f32[1,1]{1,0:T(1,128)} %get-tuple-element.15.loss_in, bf16[16,16,256]{2,1,0:T(8,128)(2,1)} %get-tuple-element.16.eg_in, ...), custom_call_target="tpu_custom_call" | custom-call | tf_op jit(solution)/shard_map/write_out/pallas_call | solution.py:591

commit v2 on v1

--- a/solution.py
+++ b/solution.py
@@ -63,6 +63,12 @@
             device_id=(s, e), device_id_type=MESH,
         )
 
+    def all_in(ref, sem):
+        remote(ref, ref, sem, sem, me_s, epeer(1)).wait_recv()
+
+    def all_out(ref, sem):
+        drains.append(lambda: remote(ref, ref, sem, sem, me_s, epeer(1)).wait_send())
+
     def loop(lo, hi, fn):
         def step(i, carry):
             fn(i)
@@ -161,7 +167,7 @@
     loop(0, ne, put_labels)
 
     def lab_copy(at, e):
-        return remote(lab_snd.at[e], lab_rcv.at[at], lab_s.at[e], lab_r.at[at], me_s, e)
+        return remote(lab_snd.at[e], lab_rcv.at[at], lab_s.at[0], lab_r.at[0], me_s, e)
 
     loop(1, ne, lambda k: lab_copy(me_e, epeer(k)).start())
     lab_rcv[pl.ds(me_e, 1)] = lab_snd[pl.ds(me_e, 1)]
@@ -173,7 +179,7 @@
                 halo_copy(d, me_s + ds, me_e + de).wait_send()
 
     drains.append(drain_halo)
-    drains.append(lambda: loop(1, ne, lambda k: lab_copy(me_e, epeer(k)).wait_send()))
+    all_out(lab_snd.at[pl.ds(0, ne - 1)], lab_s.at[0])
 
     for load in loads[3:]:
         load.wait()
@@ -239,11 +245,11 @@
     half = ne // 2
 
     def turn(i):
-        m = (i + 1) // 2
-        return half + m * (1 - 2 * lax.rem(i, 2))
+        m = i // 2 + 1
+        return jnp.where(lax.rem(i, 2) == 0, m, ne - m)
 
     def row_copy(at, e):
-        return remote(row_snd.at[e], row_rcv.at[at], row_s.at[e], row_r.at[at], me_s, e)
+        return remote(row_snd.at[e], row_rcv.at[at], row_s.at[0], row_r.at[at], me_s, e)
 
     def dispatch(i):
         e = epeer(turn(i))
@@ -252,7 +258,7 @@
         row_copy(me_e, e).start()
 
     loop(0, ne - 1, dispatch)
-    drains.append(lambda: loop(1, ne, lambda k: row_copy(me_e, epeer(k)).wait_send()))
+    all_out(row_snd.at[pl.ds(0, ne - 1)], row_s.at[0])
     row_rcv[me_e, 0] = act[inv[2 * me_e]]
     row_rcv[me_e, 1] = act[inv[2 * me_e + 1]]
 
@@ -284,7 +290,6 @@
         acc_m[...] = tm
 
     def arrived(s):
-        lab_copy(s, s).wait_recv()
         row_copy(s, s).wait_recv()
 
     forward(me_e)
@@ -295,6 +300,7 @@
         arrived(behind)
         forward(before, behind)
 
+    all_in(lab_rcv.at[pl.ds(0, ne - 1)], lab_r.at[0])
     loop(1, half, forward_turn)
     arrived(epeer(half))
     forward(epeer(half))
@@ -307,20 +313,20 @@
         axis=0,
     )[None]
 
-    def st1_copy(at, e, k):
-        return remote(st1.at[at], st1.at[at], st1_s.at[k], st1_r.at[at], me_s, e)
-
-    loop(1, ne, lambda k: st1_copy(me_e, epeer(k), k).start())
-    drains.append(lambda: loop(1, ne, lambda k: st1_copy(me_e, epeer(k), k).wait_send()))
-    loop(1, ne, lambda k: st1_copy(epeer(k), epeer(k), k).wait_recv())
+    def st1_copy(e):
+        return remote(st1.at[me_e], st1.at[me_e], st1_s.at[0], st1_r.at[0], me_s, e)
+
+    loop(1, ne, lambda k: st1_copy(epeer(k)).start())
+    all_out(st1.at[pl.ds(0, ne - 1)], st1_s.at[0])
+    all_in(st1.at[pl.ds(0, ne - 1)], st1_r.at[0])
     st2[pl.ds(me_s, 1)] = jnp.sum(st1[...], axis=0)[None]
 
-    def st2_copy(at, s, k):
-        return remote(st2.at[at], st2.at[at], st2_s.at[k], st2_r.at[at], s, me_e)
-
-    loop(1, ns, lambda k: st2_copy(me_s, speer(k), k).start())
-    drains.append(lambda: loop(1, ns, lambda k: st2_copy(me_s, speer(k), k).wait_send()))
-    loop(1, ns, lambda k: st2_copy(speer(k), speer(k), k).wait_recv())
+    def st2_copy(s):
+        return remote(st2.at[me_s], st2.at[me_s], st2_s.at[0], st2_r.at[0], s, me_e)
+
+    loop(1, ns, lambda k: st2_copy(speer(k)).start())
+    all_out(st2.at[pl.ds(0, ns - 1)], st2_s.at[0])
+    all_in(st2.at[pl.ds(0, ns - 1)], st2_r.at[0])
     sums = jnp.sum(st2[...], axis=0)
 
     voxels = ns * ne * ROWS * W
@@ -359,7 +365,7 @@
         acc_g[...] = tg
 
     def ret_copy(at, e):
-        return remote(ret_snd.at[e], ret_rcv.at[at], ret_s.at[e], ret_r.at[at], me_s, e)
+        return remote(ret_snd.at[e], ret_rcv.at[at], ret_s.at[0], ret_r.at[0], me_s, e)
 
     def backward_turn(i):
         k = half - i
@@ -371,7 +377,7 @@
     backward(ret_snd, epeer(half))
     ret_copy(me_e, epeer(half)).start()
     loop(1, half, backward_turn)
-    drains.append(lambda: loop(1, ne, lambda k: ret_copy(me_e, epeer(k)).wait_send()))
+    all_out(ret_snd.at[pl.ds(0, ne - 1)], ret_s.at[0])
     backward(ret_rcv, me_e)
 
     egf[:, 0:8, :] = dot(gl_all[...], ha_all[...], NT).reshape(GROWS, 8, HID)
@@ -386,13 +392,13 @@
     own = GROWS // ns
 
     def eg_copy(at, s):
-        return remote(eg_snd.at[pl.ds(s * own, own)], eg_rcv.at[at], eg_s.at[s], eg_r.at[at], s, me_e)
+        return remote(eg_snd.at[pl.ds(s * own, own)], eg_rcv.at[at], eg_s.at[0], eg_r.at[0], s, me_e)
 
     loop(1, ns, lambda k: eg_copy(me_s, speer(k)).start())
-    drains.append(lambda: loop(1, ns, lambda k: eg_copy(me_s, speer(k)).wait_send()))
+    all_out(eg_rcv.at[pl.ds(0, ns - 1)], eg_s.at[0])
     eg_rcv[pl.ds(me_s, 1)] = eg_snd[pl.ds(me_s * own, own)][None]
 
-    loop(1, ne, lambda k: ret_copy(epeer(k), epeer(k)).wait_recv())
+    all_in(ret_rcv.at[pl.ds(0, ne - 1)], ret_r.at[0])
     gp3[96:, :] = jnp.zeros((CLS - 96, ROWS * W), BF16)
 
     def conv_back(r):
@@ -413,44 +419,44 @@
     gka_snd[...] = full.astype(BF16).reshape(GROWS, 16, CLS)
 
     def gka_copy(at, s):
-        return remote(gka_snd.at[pl.ds(s * own, own)], gka_rcv.at[at], gka_s.at[s], gka_r.at[at], s, me_e)
+        return remote(gka_snd.at[pl.ds(s * own, own)], gka_rcv.at[at], gka_s.at[0], gka_r.at[0], s, me_e)
 
     loop(1, ns, lambda k: gka_copy(me_s, speer(k)).start())
-    drains.append(lambda: loop(1, ns, lambda k: gka_copy(me_s, speer(k)).wait_send()))
+    all_out(gka_rcv.at[pl.ds(0, ns - 1)], gka_s.at[0])
     gka_rcv[pl.ds(me_s, 1)] = gka_snd[pl.ds(me_s * own, own)][None]
 
-    loop(1, ns, lambda k: eg_copy(speer(k), speer(k)).wait_recv())
+    all_in(eg_rcv.at[pl.ds(0, ns - 1)], eg_r.at[0])
     eg_all[pl.ds(me_s * own, own)] = jnp.sum(eg_rcv[...].astype(F32), axis=0).astype(BF16)
 
-    def ega_copy(at, s, k):
-        part = eg_all.at[pl.ds(at * own, own)]
-        return remote(part, part, ega_s.at[k], ega_r.at[at], s, me_e)
-
-    loop(1, ns, lambda k: ega_copy(me_s, speer(k), k).start())
-    drains.append(lambda: loop(1, ns, lambda k: ega_copy(me_s, speer(k), k).wait_send()))
-
-    loop(1, ns, lambda k: gka_copy(speer(k), speer(k)).wait_recv())
+    def ega_copy(s):
+        part = eg_all.at[pl.ds(me_s * own, own)]
+        return remote(part, part, ega_s.at[0], ega_r.at[0], s, me_e)
+
+    loop(1, ns, lambda k: ega_copy(speer(k)).start())
+    all_out(eg_all.at[pl.ds(0, (ns - 1) * own)], ega_s.at[0])
+
+    all_in(gka_rcv.at[pl.ds(0, ns - 1)], gka_r.at[0])
     gkb[pl.ds(me_e, 1)] = jnp.sum(gka_rcv[...].astype(F32), axis=0).astype(BF16)[None]
 
-    def gkb_copy(at, e, k):
-        return remote(gkb.at[at], gkb.at[at], gkb_s.at[k], gkb_r.at[at], me_s, e)
-
-    loop(1, ne, lambda k: gkb_copy(me_e, epeer(k), k).start())
-    drains.append(lambda: loop(1, ne, lambda k: gkb_copy(me_e, epeer(k), k).wait_send()))
-    loop(1, ne, lambda k: gkb_copy(epeer(k), epeer(k), k).wait_recv())
+    def gkb_copy(e):
+        return remote(gkb.at[me_e], gkb.at[me_e], gkb_s.at[0], gkb_r.at[0], me_s, e)
+
+    loop(1, ne, lambda k: gkb_copy(epeer(k)).start())
+    all_out(gkb.at[pl.ds(0, ne - 1)], gkb_s.at[0])
+    all_in(gkb.at[pl.ds(0, ne - 1)], gkb_r.at[0])
     gkc[pl.ds(me_s * own, own)] = jnp.sum(gkb[...].astype(F32), axis=0).astype(BF16)
 
-    def gkc_copy(at, s, k):
-        part = gkc.at[pl.ds(at * own, own)]
-        return remote(part, part, gkc_s.at[k], gkc_r.at[at], s, me_e)
-
-    loop(1, ns, lambda k: gkc_copy(me_s, speer(k), k).start())
-    drains.append(lambda: loop(1, ns, lambda k: gkc_copy(me_s, speer(k), k).wait_send()))
-    loop(1, ns, lambda k: ega_copy(speer(k), speer(k), k).wait_recv())
+    def gkc_copy(s):
+        part = gkc.at[pl.ds(me_s * own, own)]
+        return remote(part, part, gkc_s.at[0], gkc_r.at[0], s, me_e)
+
+    loop(1, ns, lambda k: gkc_copy(speer(k)).start())
+    all_out(gkc.at[pl.ds(0, (ns - 1) * own)], gkc_s.at[0])
+    all_in(eg_all.at[pl.ds(0, (ns - 1) * own)], ega_r.at[0])
     stores[0].start()
     stores[1].start()
 
-    loop(1, ns, lambda k: gkc_copy(speer(k), speer(k), k).wait_recv())
+    all_in(gkc.at[pl.ds(0, (ns - 1) * own)], gkc_r.at[0])
     stores[2].start()
     for drain in drains:
         drain()
@@ -561,7 +567,7 @@
         V((ne, own, 16, CLS), BF16),
         V((GROWS, 16, CLS), BF16),
     ]
-    sems = [8, 8, ne, ne, ne, ne, ne, ne, ns, ns, ne, ne, ns, ns, ns, ns, ns, ns, ne, ne, ns, ns]
+    sems = [8, 8, 1, 1, 1, ne] + [1] * 16
     scratch += [pltpu.SemaphoreType.DMA((n,)) for n in sems]
     hbm = pl.BlockSpec(memory_space=pltpu.HBM)
     outs = pl.pallas_call(

time: 68.6 us -> 62.9 us (0.917)
  Pallas kernels: 67.9 us -> 62.1 us
    pallas_call x1, Pallas kernels: 65.4 us -> 59.7 us  [on_device(): pl.pallas_call(functools.partial(body, ns, ne), out_shape=[jax.ShapeDtype...]
where the time goes in v2:
time: 62.9 us; the launch traced here: 62.8 us
  Pallas kernels  62.1 us (99%)
  between operations  0.64 us (1%)
    pallas_call x1, Pallas kernels, on_device(): pl.pallas_call(functools.partial(body, ns, ne), out_shape=[jax.ShapeDtype...  59.7 us
    pallas_call x1, Pallas kernels, on_device(): pl.pallas_call(write_out, out_shape=[jax.ShapeDtypeStruct((1, 1), F32), j...  2.47 us

profile of v2, /device:TPU:1, one launch (start us, length us, event | category | flops | bytes accessed | tf_op | source)
XLA Modules:
  0.0 62.8 jit_solution(11385852981301764742)
XLA Ops:
  0.6 59.7 %fused_head.1 = (f32[1,1]{1,0:T(1,128)}, bf16[16,16,256]{2,1,0:T(8,128)(2,1)}, bf16[16,16,128]{2,1,0:T(8,128)(2,1)}) custom-call(bf16[512,128]{1,0:T(8,128)(2,1)} %bitcast.12, bf16[27,32,32]{2,1,0:T(8,128)(2,1)} %k_hbm.1, s32[16,128]{1,0:T(8,128)} %bitcast.15, s32[16]{0:T(128)} %bitcast.16, bf16[32,256]{1,0:T(8,128)(2,1)} %bitcast.14, ...), custom_call_target="tpu_custom_call" | custom-call | tf_op jit(solution)/shard_map/fused_head/pallas_call | solution.py:573
  60.3 2.5 %write_out.1 = (f32[1,1]{1,0:T(1,128)}, f32[27,32,32]{2,1,0:T(8,128)}, f32[32,256]{1,0:T(8,128)}, f32[1,256]{1,0:T(1,128)}, f32[117,1,256]{2,1,0:T(1,128)}, /*index=5*/f32[1,117]{1,0:T(1,128)}) custom-call(f32[1,1]{1,0:T(1,128)} %get-tuple-element.15.loss_in, bf16[16,16,256]{2,1,0:T(8,128)(2,1)} %get-tuple-element.16.eg_in, ...), custom_call_target="tpu_custom_call" | custom-call | tf_op jit(solution)/shard_map/write_out/pallas_call | solution.py:597

commit v3 on v2

--- a/solution.py
+++ b/solution.py
@@ -26,7 +26,7 @@
 NT = (((1,), (1,)), ((), ()))
 NN = (((1,), (0,)), ((), ()))
 
-HALO = tuple((ds, de) for ds in (-1, 0, 1) for de in (-1, 0, 1) if (ds, de) != (0, 0))
+HALO = ((-1, 0), (1, 0), (-1, -1), (-1, 1), (1, -1), (1, 1), (0, -1), (0, 1))
 
 
 def dot(a, b, dims=NN):
@@ -75,6 +75,23 @@
             return carry
         lax.fori_loop(lo, hi, step, 0)
 
+    half = ne // 2
+    far_e = sorted(range(1, ne), key=lambda k: -min(k, ne - k))
+    grid = (4, ns // 4) if ns % 4 == 0 else (1, ns)
+    far_s = sorted(
+        ((a, b) for a in range(grid[0]) for b in range(grid[1]) if a or b),
+        key=lambda p: -min(p[0], grid[0] - p[0]) - min(p[1], grid[1] - p[1]),
+    )
+
+    def each_e(fn):
+        for k in far_e:
+            fn(epeer(k))
+
+    def each_s(fn):
+        row, col = me_s // grid[1], lax.rem(me_s, grid[1])
+        for a, b in far_s:
+            fn(lax.rem(row + a, grid[0]) * grid[1] + lax.rem(col + b, grid[1]))
+
     def epeer(k):
         return lax.rem(me_e + k, ne)
 
@@ -109,8 +126,8 @@
             xp[z, h] = jnp.zeros((C, W), BF16)
 
     barrier = pltpu.get_barrier_semaphore()
-    loop(1, ne, lambda k: pl.semaphore_signal(barrier, 1, device_id=(me_s, epeer(k)), device_id_type=MESH))
-    loop(1, ns, lambda k: pl.semaphore_signal(barrier, 1, device_id=(speer(k), me_e), device_id_type=MESH))
+    each_e(lambda e: pl.semaphore_signal(barrier, 1, device_id=(me_s, e), device_id_type=MESH))
+    each_s(lambda s: pl.semaphore_signal(barrier, 1, device_id=(s, me_e), device_id_type=MESH))
     for ds, de in HALO:
         if ds and de:
             @pl.when(exists(ds, de))
@@ -212,6 +229,7 @@
         acc_c[...] += jnp.where(classes == lab_ext[pl.ds(r, 1), :], 1.0, 0.0)
 
     loop(0, ROWS, count)
+    x9[TAPS * C:, :] = jnp.zeros((96, ROWS * W), BF16)
 
     for d, (ds, de) in enumerate(HALO):
         @pl.when(exists(-ds, -de))
@@ -229,7 +247,7 @@
 
     def conv(p):
         lane = slice(p * BLK, (p + 1) * BLK)
-        out = dot(kw[...], x9[:, lane])
+        out = dot(kw[...], x9[0:TAPS * C, lane])
         for j in range(2):
             part = out[:, j * W:(j + 1) * W]
             left = jnp.where(lanes > 0, pltpu.roll(part[0:C], 1, 1), 0.0)
@@ -241,8 +259,6 @@
 
     for p in range(ROWS // 2):
         conv(p)
-
-    half = ne // 2
 
     def turn(i):
         m = i // 2 + 1
@@ -316,7 +332,7 @@
     def st1_copy(e):
         return remote(st1.at[me_e], st1.at[me_e], st1_s.at[0], st1_r.at[0], me_s, e)
 
-    loop(1, ne, lambda k: st1_copy(epeer(k)).start())
+    each_e(lambda e: st1_copy(e).start())
     all_out(st1.at[pl.ds(0, ne - 1)], st1_s.at[0])
     all_in(st1.at[pl.ds(0, ne - 1)], st1_r.at[0])
     st2[pl.ds(me_s, 1)] = jnp.sum(st1[...], axis=0)[None]
@@ -324,7 +340,7 @@
     def st2_copy(s):
         return remote(st2.at[me_s], st2.at[me_s], st2_s.at[0], st2_r.at[0], s, me_e)
 
-    loop(1, ns, lambda k: st2_copy(speer(k)).start())
+    each_s(lambda s: st2_copy(s).start())
     all_out(st2.at[pl.ds(0, ns - 1)], st2_s.at[0])
     all_in(st2.at[pl.ds(0, ns - 1)], st2_r.at[0])
     sums = jnp.sum(st2[...], axis=0)
@@ -357,9 +373,9 @@
                 parts.append(g.astype(BF16))
             gl = jnp.concatenate(parts, axis=1)
             gl_all[:, col] = gl
-            gh = (dot(w2t[...], gl) * d_all[:, col]).astype(BF16)
-            gh_all[:, col] = gh
-            gx = dot(w1t[...], gh).astype(BF16)
+            for c in range(0, HID, 64):
+                gh_all[c:c + 64, col] = (dot(w2t[c:c + 64, :], gl) * d_all[c:c + 64, col]).astype(BF16)
+            gx = dot(w1t[...], gh_all[:, col]).astype(BF16)
             dst[s, 0] = gx[:, 0:W]
             dst[s, 1] = gx[:, W:]
         acc_g[...] = tg
@@ -399,7 +415,6 @@
     eg_rcv[pl.ds(me_s, 1)] = eg_snd[pl.ds(me_s * own, own)][None]
 
     all_in(ret_rcv.at[pl.ds(0, ne - 1)], ret_r.at[0])
-    gp3[96:, :] = jnp.zeros((CLS - 96, ROWS * W), BF16)
 
     def conv_back(r):
         lane = slice(r * W, (r + 1) * W)
@@ -412,18 +427,29 @@
 
     for r in range(ROWS):
         conv_back(r)
-    gkt = dot(x9[...], gp3[...], NT)
-    rest = jnp.concatenate([pltpu.roll(gkt[216:], 96 - c * C, 1) for c in range(3)], axis=0)
-    full = jnp.where(lax.broadcasted_iota(I32, (216, CLS), 1) < 96, gkt[0:216], rest)
-    full = jnp.concatenate([full, jnp.zeros((40, CLS), F32)], axis=0)
+    gkt = dot(gp3[...], x9[...], NT)
+    tail = gkt[:, 256:]
+    rest = tail[0:24]
+    for g in range(1, 4):
+        rest = rest + pltpu.roll(tail[24 * g:24 * g + 24], C * g, 1)
+    full = jnp.concatenate([gkt[:, 0:128], gkt[:, 128:256], rest, jnp.zeros((40, CLS), F32)], axis=0)
     gka_snd[...] = full.astype(BF16).reshape(GROWS, 16, CLS)
 
     def gka_copy(at, s):
         return remote(gka_snd.at[pl.ds(s * own, own)], gka_rcv.at[at], gka_s.at[0], gka_r.at[0], s, me_e)
 
-    loop(1, ns, lambda k: gka_copy(me_s, speer(k)).start())
+    each_s(lambda s: gka_copy(me_s, s).start())
     all_out(gka_rcv.at[pl.ds(0, ns - 1)], gka_s.at[0])
     gka_rcv[pl.ds(me_s, 1)] = gka_snd[pl.ds(me_s * own, own)][None]
+
+    all_in(gka_rcv.at[pl.ds(0, ns - 1)], gka_r.at[0])
+    gkb[pl.ds(me_e, 1)] = jnp.sum(gka_rcv[...].astype(F32), axis=0).astype(BF16)[None]
+
+    def gkb_copy(e):
+        return remote(gkb.at[me_e], gkb.at[me_e], gkb_s.at[0], gkb_r.at[0], me_s, e)
+
+    each_e(lambda e: gkb_copy(e).start())
+    all_out(gkb.at[pl.ds(0, ne - 1)], gkb_s.at[0])
 
     all_in(eg_rcv.at[pl.ds(0, ns - 1)], eg_r.at[0])
     eg_all[pl.ds(me_s * own, own)] = jnp.sum(eg_rcv[...].astype(F32), axis=0).astype(BF16)
@@ -435,14 +461,6 @@
     loop(1, ns, lambda k: ega_copy(speer(k)).start())
     all_out(eg_all.at[pl.ds(0, (ns - 1) * own)], ega_s.at[0])
 
-    all_in(gka_rcv.at[pl.ds(0, ns - 1)], gka_r.at[0])
-    gkb[pl.ds(me_e, 1)] = jnp.sum(gka_rcv[...].astype(F32), axis=0).astype(BF16)[None]
-
-    def gkb_copy(e):
-        return remote(gkb.at[me_e], gkb.at[me_e], gkb_s.at[0], gkb_r.at[0], me_s, e)
-
-    loop(1, ne, lambda k: gkb_copy(epeer(k)).start())
-    all_out(gkb.at[pl.ds(0, ne - 1)], gkb_s.at[0])
     all_in(gkb.at[pl.ds(0, ne - 1)], gkb_r.at[0])
     gkc[pl.ds(me_s * own, own)] = jnp.sum(gkb[...].astype(F32), axis=0).astype(BF16)
 
@@ -450,7 +468,7 @@
         part = gkc.at[pl.ds(me_s * own, own)]
         return remote(part, part, gkc_s.at[0], gkc_r.at[0], s, me_e)
 
-    loop(1, ns, lambda k: gkc_copy(speer(k)).start())
+    each_s(lambda s: gkc_copy(s).start())
     all_out(gkc.at[pl.ds(0, (ns - 1) * own)], gkc_s.at[0])
     all_in(eg_all.at[pl.ds(0, (ns - 1) * own)], ega_r.at[0])
     stores[0].start()
@@ -474,14 +492,11 @@
         load.start()
     loads[0].wait()
     full = gkc[...].astype(F32).reshape(GROWS * 16, CLS)
-    lanes = lax.broadcasted_iota(I32, (72, CLS), 1)
-    rest = pltpu.roll(full[0:72], C, 1)
-    for c in (1, 2):
-        rest = jnp.where(lanes < c * C, rest, pltpu.roll(full[c * 72:(c + 1) * 72], (c + 1) * C, 1))
-    gkt = jnp.concatenate([full[0:216], rest], axis=0)
+    rest = jnp.concatenate([full[192:216]] + [pltpu.roll(full[192:216], CLS - C * g, 1) for g in range(1, 4)], axis=0)
     for j in range(TAPS):
-        turned = gkt[j * C:(j + 1) * C]
-        turned = jnp.concatenate([turned, jnp.zeros((CLS - C, CLS), F32)], axis=0).T
+        turned = full[j // 4 * 96:j // 4 * 96 + 96] if j < 8 else rest
+        if j % 4:
+            turned = pltpu.roll(turned, CLS - C * (j % 4), 1)
         for c in range(3):
             gk[3 * j + c] = turned[c * C:(c + 1) * C, 0:C]
     pairs = ((gk, gk_out), (gw1, gw1_out), (gb1, gb1_out), (gw2, gw2_out.at[:, 0, :]), (gb2, gb2_out), (loss, loss_out))
@@ -526,7 +541,7 @@
         V((4, 10, C, W), BF16),
         V((3 * C, TAPS * C), F32),
         V((3 * C, TAPS * C), BF16),
-        V((TAPS * C, ROWS * W), BF16),
+        V((384, ROWS * W), BF16),
         V((ROWS + 1, C, W), BF16),
         V((ROWS, C, W), F32),
         V((ROWS + 8, W), I32),
@@ -561,7 +576,7 @@
         V((GROWS, 16, HID), BF16),
         V((ns, own, 16, HID), BF16),
         V((GROWS, 16, HID), BF16),
-        V((CLS, ROWS * W), BF16),
+        V((96, ROWS * W), BF16),
         V((GROWS, 16, CLS), BF16),
         V((ns, own, 16, CLS), BF16),
         V((ne, own, 16, CLS), BF16),

time: 62.9 us -> 61.9 us (0.984)
  Pallas kernels: 62.1 us -> 61.2 us
    pallas_call x1, Pallas kernels: 59.7 us -> 58.8 us  [on_device(): pl.pallas_call(functools.partial(body, ns, ne), out_shape=[jax.ShapeDtype...]
where the time goes in v3:
time: 61.9 us; the launch traced here: 61.8 us
  Pallas kernels  61.2 us (99%)
  between operations  0.64 us (1%)
    pallas_call x1, Pallas kernels, on_device(): pl.pallas_call(functools.partial(body, ns, ne), out_shape=[jax.ShapeDtype...  58.8 us
    pallas_call x1, Pallas kernels, on_device(): pl.pallas_call(write_out, out_shape=[jax.ShapeDtypeStruct((1, 1), F32), j...  2.4 us

profile of v3, /device:TPU:1, one launch (start us, length us, event | category | flops | bytes accessed | tf_op | source)
XLA Modules:
  0.0 61.8 jit_solution(3982694261049105958)
XLA Ops:
  0.6 58.8 %fused_head.1 = (f32[1,1]{1,0:T(1,128)}, bf16[16,16,256]{2,1,0:T(8,128)(2,1)}, bf16[16,16,128]{2,1,0:T(8,128)(2,1)}) custom-call(bf16[512,128]{1,0:T(8,128)(2,1)} %bitcast.12, bf16[27,32,32]{2,1,0:T(8,128)(2,1)} %k_hbm.1, s32[16,128]{1,0:T(8,128)} %bitcast.15, s32[16]{0:T(128)} %bitcast.16, bf16[32,256]{1,0:T(8,128)(2,1)} %bitcast.14, ...), custom_call_target="tpu_custom_call" | custom-call | tf_op jit(solution)/shard_map/fused_head/pallas_call | solution.py:588
  59.4 2.4 %write_out.1 = (f32[1,1]{1,0:T(1,128)}, f32[27,32,32]{2,1,0:T(8,128)}, f32[32,256]{1,0:T(8,128)}, f32[1,256]{1,0:T(1,128)}, f32[117,1,256]{2,1,0:T(1,128)}, /*index=5*/f32[1,117]{1,0:T(1,128)}) custom-call(f32[1,1]{1,0:T(1,128)} %get-tuple-element.15.loss_in, bf16[16,16,256]{2,1,0:T(8,128)(2,1)} %get-tuple-element.16.eg_in, ...), custom_call_target="tpu_custom_call" | custom-call | tf_op jit(solution)/shard_map/write_out/pallas_call | solution.py:612

commit v4 on v3

--- a/solution.py
+++ b/solution.py
@@ -112,8 +112,7 @@
         (w1_hbm, w1_ref), (b1_hbm, b1_ref), (w2_hbm, w2_ref), (b2_hbm, b2_ref),
     )
     loads = [pltpu.make_async_copy(src, dst, in_sem.at[i]) for i, (src, dst) in enumerate(pairs)]
-    for load in loads:
-        load.start()
+    loads[0].start()
 
     results = ((loss_ref, loss_out), (eg_all, eg_out), (gkc, gkc_out))
     stores = [pltpu.make_async_copy(src, dst, out_sem.at[i]) for i, (src, dst) in enumerate(results)]
@@ -126,13 +125,22 @@
             xp[z, h] = jnp.zeros((C, W), BF16)
 
     barrier = pltpu.get_barrier_semaphore()
-    each_e(lambda e: pl.semaphore_signal(barrier, 1, device_id=(me_s, e), device_id_type=MESH))
-    each_s(lambda s: pl.semaphore_signal(barrier, 1, device_id=(s, me_e), device_id_type=MESH))
+    def hello(s, e):
+        pl.semaphore_signal(barrier, 1, device_id=(s, e), device_id_type=MESH)
+
+    hellos = []
+    each_e(lambda e: hellos.append((me_s, e)))
+    each_s(lambda s: hellos.append((s, me_e)))
+    for i in range(ne - 1 + ns - 1):
+        at = i // 2 if i % 2 == 0 else ne - 1 + i // 2
+        hello(*hellos[at if ns == ne else i])
     for ds, de in HALO:
         if ds and de:
             @pl.when(exists(ds, de))
             def _():
-                pl.semaphore_signal(barrier, 1, device_id=(me_s + ds, me_e + de), device_id_type=MESH)
+                hello(me_s + ds, me_e + de)
+    for load in loads[1:]:
+        load.start()
     n_s = (me_s > 0).astype(I32) + (me_s < ns - 1).astype(I32)
     n_e = (me_e > 0).astype(I32) + (me_e < ne - 1).astype(I32)
 
@@ -281,29 +289,38 @@
     ones = jnp.where(lax.broadcasted_iota(I32, (16, BLK), 0) == 0, 1.0, 0.0).astype(BF16)
 
     def forward(*blocks):
-        ti = acc_i[...]
-        tm = acc_m[...]
+        xas, cols = [], []
         for s in blocks:
             col = pl.ds(pl.multiple_of(s * BLK, BLK), BLK)
             x = row_rcv[s]
             xa = jnp.concatenate([jnp.concatenate([x[0], x[1]], axis=1), ones], axis=0)
             xa_all[:, col] = xa
-            v = dot(w1a[:, 0:48], xa)
+            xas.append(xa)
+            cols.append(col)
+        xa = jnp.concatenate(xas, axis=1)
+        has = []
+        for c in range(0, HID, 64):
+            v = dot(w1a[c:c + 64, 0:48], xa)
             t = jnp.tanh(v)
             ha = (v + v * t).astype(BF16)
-            ha_all[:, col] = ha
-            d_all[:, col] = (1.0 + t) + v * (1.0 - t * t)
-            z = dot(w2h[...], ha)
-            lab = lab_rcv[s]
-            for j in range(CAP):
-                lj = lab[j:j + 1, :]
-                t2 = jnp.tanh(z[:, j * W:(j + 1) * W] + b2bc[...])
-                t2 = jnp.where(lj < 0, 1.0, t2)
-                q_all[:, pl.ds(pl.multiple_of(s * BLK + j * W, W), W)] = 1.0 - t2 * t2
-                ti = ti + jnp.where(classes == lj, t2, 0.0)
-                tm = tm + t2
-        acc_i[...] = ti
-        acc_m[...] = tm
+            d = (1.0 + t) + v * (1.0 - t * t)
+            for n, col in enumerate(cols):
+                ha_all[c:c + 64, col] = ha[:, n * BLK:(n + 1) * BLK]
+                d_all[c:c + 64, col] = d[:, n * BLK:(n + 1) * BLK]
+            has.append(ha)
+        ha = jnp.concatenate(has, axis=0)
+        for c in (0, 64):
+            z = dot(w2h[c:c + 64, :], ha)
+            for n, s in enumerate(blocks):
+                lab = lab_rcv[s]
+                for j in range(CAP):
+                    lj = lab[j:j + 1, :]
+                    at = n * BLK + j * W
+                    t2 = jnp.tanh(z[:, at:at + W] + b2bc[c:c + 64, :])
+                    t2 = jnp.where(lj < 0, 1.0, t2)
+                    q_all[c:c + 64, pl.ds(pl.multiple_of(s * BLK + j * W, W), W)] = 1.0 - t2 * t2
+                    acc_i[c:c + 64, :] += jnp.where(classes[c:c + 64] == lj, t2, 0.0)
+                    acc_m[c:c + 64, :] += t2
 
     def arrived(s):
         row_copy(s, s).wait_recv()
@@ -361,6 +378,7 @@
 
     def backward(dst, *blocks):
         tg = acc_g[...]
+        gls, cols = [], []
         for s in blocks:
             col = pl.ds(pl.multiple_of(s * BLK, BLK), BLK)
             lab = lab_rcv[s]
@@ -373,11 +391,23 @@
                 parts.append(g.astype(BF16))
             gl = jnp.concatenate(parts, axis=1)
             gl_all[:, col] = gl
-            for c in range(0, HID, 64):
-                gh_all[c:c + 64, col] = (dot(w2t[c:c + 64, :], gl) * d_all[c:c + 64, col]).astype(BF16)
-            gx = dot(w1t[...], gh_all[:, col]).astype(BF16)
-            dst[s, 0] = gx[:, 0:W]
-            dst[s, 1] = gx[:, W:]
+            gls.append(gl)
+            cols.append(col)
+        gl = jnp.concatenate(gls, axis=1)
+        ghs = []
+        for c in range(0, HID, 64):
+            g = dot(w2t[c:c + 64, :], gl)
+            gh = jnp.concatenate(
+                [(g[:, n * BLK:(n + 1) * BLK] * d_all[c:c + 64, col]).astype(BF16) for n, col in enumerate(cols)],
+                axis=1,
+            )
+            for n, col in enumerate(cols):
+                gh_all[c:c + 64, col] = gh[:, n * BLK:(n + 1) * BLK]
+            ghs.append(gh)
+        gx = dot(w1t[...], jnp.concatenate(ghs, axis=0)).astype(BF16)
+        for n, s in enumerate(blocks):
+            dst[s, 0] = gx[:, n * BLK:n * BLK + W]
+            dst[s, 1] = gx[:, n * BLK + W:(n + 1) * BLK]
         acc_g[...] = tg
 
     def ret_copy(at, e):
@@ -396,6 +426,35 @@
     all_out(ret_snd.at[pl.ds(0, ne - 1)], ret_s.at[0])
     backward(ret_rcv, me_e)
 
+    all_in(ret_rcv.at[pl.ds(0, ne - 1)], ret_r.at[0])
+
+    def conv_back(r):
+        lane = slice(r * W, (r + 1) * W)
+        e = ids_ref[r]
+        j = jnp.where(inv[2 * e] == r, 0, 1)
+        gp = (ret_rcv[e, j].astype(F32) * dconv[r]).astype(BF16).astype(F32)
+        gp3[0:C, lane] = jnp.where(lanes < W - 1, pltpu.roll(gp, W - 1, 1), 0.0).astype(BF16)
+        gp3[C:2 * C, lane] = gp.astype(BF16)
+        gp3[2 * C:3 * C, lane] = jnp.where(lanes > 0, pltpu.roll(gp, 1, 1), 0.0).astype(BF16)
+
+    for r in range(ROWS):
+        conv_back(r)
+    gkt = dot(gp3[...], x9[...], NT)
+    tail = gkt[:, 256:]
+    rest = tail[0:24]
+    for g in range(1, 4):
+        rest = rest + pltpu.roll(tail[24 * g:24 * g + 24], C * g, 1)
+    full = jnp.concatenate([gkt[:, 0:128], gkt[:, 128:256], rest, jnp.zeros((40, CLS), F32)], axis=0)
+    gka_snd[...] = full.astype(BF16).reshape(GROWS, 16, CLS)
+
+    own = GROWS // ns
+
+    def gka_copy(at, s):
+        return remote(gka_snd.at[pl.ds(s * own, own)], gka_rcv.at[at], gka_s.at[0], gka_r.at[0], s, me_e)
+
+    each_s(lambda s: gka_copy(me_s, s).start())
+    all_out(gka_rcv.at[pl.ds(0, ns - 1)], gka_s.at[0])
+    gka_rcv[pl.ds(me_s, 1)] = gka_snd[pl.ds(me_s * own, own)][None]
     egf[:, 0:8, :] = dot(gl_all[...], ha_all[...], NT).reshape(GROWS, 8, HID)
     gw1 = dot(xa_all[...], gh_all[...], NT)
     for i in range(GROWS):
@@ -405,7 +464,6 @@
     gb2 = lane_row(acc_g[...])
     egf[0, 11:12, 0:CLS] = gb2
     eg_snd[...] = egf[...].astype(BF16)
-    own = GROWS // ns
 
     def eg_copy(at, s):
         return remote(eg_snd.at[pl.ds(s * own, own)], eg_rcv.at[at], eg_s.at[0], eg_r.at[0], s, me_e)
@@ -414,33 +472,6 @@
     all_out(eg_rcv.at[pl.ds(0, ns - 1)], eg_s.at[0])
     eg_rcv[pl.ds(me_s, 1)] = eg_snd[pl.ds(me_s * own, own)][None]
 
-    all_in(ret_rcv.at[pl.ds(0, ne - 1)], ret_r.at[0])
-
-    def conv_back(r):
-        lane = slice(r * W, (r + 1) * W)
-        e = ids_ref[r]
-        j = jnp.where(inv[2 * e] == r, 0, 1)
-        gp = (ret_rcv[e, j].astype(F32) * dconv[r]).astype(BF16).astype(F32)
-        gp3[0:C, lane] = jnp.where(lanes < W - 1, pltpu.roll(gp, W - 1, 1), 0.0).astype(BF16)
-        gp3[C:2 * C, lane] = gp.astype(BF16)
-        gp3[2 * C:3 * C, lane] = jnp.where(lanes > 0, pltpu.roll(gp, 1, 1), 0.0).astype(BF16)
-
-    for r in range(ROWS):
-        conv_back(r)
-    gkt = dot(gp3[...], x9[...], NT)
-    tail = gkt[:, 256:]
-    rest = tail[0:24]
-    for g in range(1, 4):
-        rest = rest + pltpu.roll(tail[24 * g:24 * g + 24], C * g, 1)
-    full = jnp.concatenate([gkt[:, 0:128], gkt[:, 128:256], rest, jnp.zeros((40, CLS), F32)], axis=0)
-    gka_snd[...] = full.astype(BF16).reshape(GROWS, 16, CLS)
-
-    def gka_copy(at, s):
-        return remote(gka_snd.at[pl.ds(s * own, own)], gka_rcv.at[at], gka_s.at[0], gka_r.at[0], s, me_e)
-
-    each_s(lambda s: gka_copy(me_s, s).start())
-    all_out(gka_rcv.at[pl.ds(0, ns - 1)], gka_s.at[0])
-    gka_rcv[pl.ds(me_s, 1)] = gka_snd[pl.ds(me_s * own, own)][None]
 
     all_in(gka_rcv.at[pl.ds(0, ns - 1)], gka_r.at[0])
     gkb[pl.ds(me_e, 1)] = jnp.sum(gka_rcv[...].astype(F32), axis=0).astype(BF16)[None]

time: 61.9 us -> 61.7 us (level)
  no operation moved by 1% of the time
where the time goes in v4:
time: 61.7 us; the launch traced here: 61.6 us
  Pallas kernels  60.9 us (99%)
  between operations  0.64 us (1%)
    pallas_call x1, Pallas kernels, on_device(): pl.pallas_call(functools.partial(body, ns, ne), out_shape=[jax.ShapeDtype...  58.5 us
    pallas_call x1, Pallas kernels, on_device(): pl.pallas_call(write_out, out_shape=[jax.ShapeDtypeStruct((1, 1), F32), j...  2.4 us

profile of v4, /device:TPU:1, one launch (start us, length us, event | category | flops | bytes accessed | tf_op | source)
XLA Modules:
  0.0 61.6 jit_solution(3018431517894003561)
XLA Ops:
  0.6 58.5 %fused_head.1 = (f32[1,1]{1,0:T(1,128)}, bf16[16,16,256]{2,1,0:T(8,128)(2,1)}, bf16[16,16,128]{2,1,0:T(8,128)(2,1)}) custom-call(bf16[512,128]{1,0:T(8,128)(2,1)} %bitcast.12, bf16[27,32,32]{2,1,0:T(8,128)(2,1)} %k_hbm.1, s32[16,128]{1,0:T(8,128)} %bitcast.15, s32[16]{0:T(128)} %bitcast.16, bf16[32,256]{1,0:T(8,128)(2,1)} %bitcast.14, ...), custom_call_target="tpu_custom_call" | custom-call | tf_op jit(solution)/shard_map/fused_head/pallas_call | solution.py:619
  59.1 2.4 %write_out.1 = (f32[1,1]{1,0:T(1,128)}, f32[27,32,32]{2,1,0:T(8,128)}, f32[32,256]{1,0:T(8,128)}, f32[1,256]{1,0:T(1,128)}, f32[117,1,256]{2,1,0:T(1,128)}, /*index=5*/f32[1,117]{1,0:T(1,128)}) custom-call(f32[1,1]{1,0:T(1,128)} %get-tuple-element.15.loss_in, bf16[16,16,256]{2,1,0:T(8,128)(2,1)} %get-tuple-element.16.eg_in, ...), custom_call_target="tpu_custom_call" | custom-call | tf_op jit(solution)/shard_map/write_out/pallas_call | solution.py:643
